TPU v7x, 768 devices: a whole 4x8x12 slice. The times are simulated.
768 devices in a mesh: outer: 48 (over y_lo, z, core), ep: 4 (over x), tp: 4 (over y_hi).
Axes of the slice: x: 4, y: 8 (y_hi: 4, y_lo: 2; y = y_hi * 2 + y_lo), z: 12, core: 2. Of those that a mesh axis runs over, the one named last changes fastest.
Arguments:
- unnormed_queries: bfloat16 [24576, 8192], P(('outer', 'ep'), 'tp'), may hold values from -100 to 100
- unnormed_keys: bfloat16 [24576, 512], P(('outer', 'ep'), 'tp'), may hold values from -100 to 100
- value: bfloat16 [24576, 512], P(('outer', 'ep'), 'tp'), may hold values from -6 to 6
- output_gradient: bfloat16 [24576, 8192], P(('outer', 'ep'), 'tp'), may hold values from -80 to 80
- segment_ids: int32 [24576], P(('outer', 'ep')), may hold values from 0 to 53, never falling along the last dimension, each value on 1 to 896 neighbouring positions
- query_norm_gain: float32 [128], replicated, may hold values from 0.5 to 5.5
- key_norm_gain: float32 [128], replicated, may hold values from 0.5 to 5.5
Outputs:
- query_grad: bfloat16 [24576, 8192], P(('outer', 'ep'), 'tp')
- raw_key_gradient: bfloat16 [24576, 512], P(('outer', 'ep'), 'tp')
- value_gradient: bfloat16 [24576, 512], P(('outer', 'ep'), 'tp')
- query_gain_grad: float32 [128], replicated
- key_gain_grad: float32 [128], replicated
Inputs may be any that keep to these rules, and one draw needn't show every extreme that they name: `segment_ids`: document numbers never fall along the tokens; each document holds at most 896 tokens, and one holds exactly 896.
All inputs are finite; a program needn't handle non-finite values.
Results may differ from a plain program's by a relative error of at most 0.0095.
The roundings to bfloat16 on the way count: a program that leaves them out, or rounds other values in their place, can miss the bound.
Values may be sent and summed in bfloat16 or wider, within the bound.
No kernel may reach another device: no remote copies, remote signals or barrier semaphores. Data moves between devices by JAX's collectives and lax.ppermute only.
A program may use at most 64 MiB of HBM per device.

v0:
```python
import math

import jax
import jax.numpy as jnp
from jax import lax
from jax.sharding import PartitionSpec as P

QUERY_HEADS = 64
HEAD_SIZE = 128


EPS = 1e-06
NEG = -1e30


def from_behind(block, axis, distance):
    devices = range(lax.axis_size(axis))
    route = [(i - distance, i) for i in devices if i - distance in devices]
    return lax.ppermute(block, axis, route)


def head_rms_norm(raw, gain):
    value_rows = raw.astype(jnp.float32)
    inverse = lax.rsqrt(jnp.mean(value_rows * value_rows, axis=-1, keepdims=True) + EPS)
    unit = value_rows * inverse
    return (unit, inverse, (unit * gain).astype(jnp.bfloat16))


def norm_backward(grad, unit, inverse, gain):
    scaled_input = grad * gain
    inner = jnp.mean(scaled_input * unit, axis=-1, keepdims=True)
    return inverse * (scaled_input - unit * inner)


def per_device(
    unnormed_queries,
    unnormed_keys,
    value,
    output_gradient,
    segment_ids,
    query_norm_gain,
    key_norm_gain,
):
    rows = unnormed_queries.shape[0]
    kv_heads = unnormed_keys.shape[1] // HEAD_SIZE
    query_groups = unnormed_queries.shape[1] // unnormed_keys.shape[1]
    scale = 1.0 / math.sqrt(HEAD_SIZE)
    seq_devices = lax.axis_size(("outer", "ep"))
    span = min(8, seq_devices // 2)
    unit_queries, query_inverse_norm, normed_queries = head_rms_norm(
        unnormed_queries.reshape(rows, kv_heads, query_groups, HEAD_SIZE), query_norm_gain
    )
    unit_keys, key_inverse_norm, normed_keys = head_rms_norm(
        unnormed_keys.reshape(rows, kv_heads, HEAD_SIZE), key_norm_gain
    )
    value_rows = value.reshape(rows, kv_heads, HEAD_SIZE)
    gradient_list = output_gradient.reshape(rows, kv_heads, query_groups, HEAD_SIZE)
    seg_mark = segment_ids.astype(jnp.bfloat16)
    key_blocks = [normed_keys]
    value_blocks = [value_rows]
    mark_blocks = [seg_mark]
    for offset in range(1, span):
        moved = from_behind((normed_keys, value_rows, seg_mark), ("outer", "ep"), offset)
        key_blocks.append(moved[0])
        value_blocks.append(moved[1])
        mark_blocks.append(moved[2])
    here = lax.axis_index(("outer", "ep"))
    local_pos = jnp.arange(rows, dtype=jnp.int32)
    q_pos = here * rows + local_pos
    seg_q = seg_mark.astype(jnp.float32)
    lives = []
    scores = []
    for offset in range(span):
        k_pos = (here - offset) * rows + local_pos
        live = seg_q[:, None] == mark_blocks[offset].astype(jnp.float32)[None, :]
        live = live & (k_pos[None, :] <= q_pos[:, None]) & (k_pos[None, :] >= 0)
        lives.append(live)
        raw_scores = (
            jnp.einsum(
                "qhgd,khd->hgqk",
                normed_queries,
                key_blocks[offset],
                preferred_element_type=jnp.float32,
            )
            * scale
        )
        scores.append(jnp.where(live, raw_scores, NEG))
    top = scores[0].max(axis=-1, keepdims=True)
    for offset in range(1, span):
        top = jnp.maximum(top, scores[offset].max(axis=-1, keepdims=True))
    total = jnp.zeros_like(top)
    for offset in range(span):
        total = total + jnp.sum(jnp.exp(scores[offset] - top), axis=-1, keepdims=True)
    attn = jnp.zeros((rows, kv_heads, query_groups, HEAD_SIZE), jnp.float32)
    for offset in range(span):
        probs_b = (jnp.exp(scores[offset] - top) / total).astype(jnp.bfloat16)
        attn = attn + jnp.einsum(
            "hgqk,khd->qhgd", probs_b, value_blocks[offset], preferred_element_type=jnp.float32
        )
    delta = jnp.transpose(jnp.sum(gradient_list.astype(jnp.float32) * attn, axis=-1), (1, 2, 0))[
        ..., None
    ]
    normed_query_gradient = jnp.zeros((rows, kv_heads, query_groups, HEAD_SIZE), jnp.float32)
    key_parts = []
    value_parts = []
    for offset in range(span):
        probs = jnp.exp(scores[offset] - top) / total
        block_probs_b = probs.astype(jnp.bfloat16)
        dv_blk = jnp.einsum(
            "hgqk,qhgd->khd", block_probs_b, gradient_list, preferred_element_type=jnp.float32
        )
        dprob = jnp.einsum(
            "qhgd,khd->hgqk",
            gradient_list,
            value_blocks[offset],
            preferred_element_type=jnp.float32,
        )
        dscore = (probs * (dprob - delta)).astype(jnp.bfloat16)
        dq_part = (
            jnp.einsum(
                "hgqk,khd->qhgd", dscore, key_blocks[offset], preferred_element_type=jnp.float32
            )
            * scale
        )
        dk_blk = (
            jnp.einsum("hgqk,qhgd->khd", dscore, normed_queries, preferred_element_type=jnp.float32)
            * scale
        )
        parts = (dq_part, dk_blk, dv_blk)
        normed_query_gradient = normed_query_gradient + parts[0]
        key_parts.append(parts[1])
        value_parts.append(parts[2])
    normed_key_gradient = key_parts[0]
    value_gradient_total = value_parts[0]
    for offset in range(1, span):
        moved = (
            from_behind(key_parts[offset].astype(jnp.bfloat16), ("outer", "ep"), -offset).astype(
                jnp.float32
            ),
            from_behind(value_parts[offset].astype(jnp.bfloat16), ("outer", "ep"), -offset).astype(
                jnp.float32
            ),
        )
        normed_key_gradient = normed_key_gradient + moved[0]
        value_gradient_total = value_gradient_total + moved[1]
    query_grad = (
        norm_backward(normed_query_gradient, unit_queries, query_inverse_norm, query_norm_gain)
        .astype(jnp.bfloat16)
        .reshape(rows, -1)
    )
    raw_key_gradient = (
        norm_backward(normed_key_gradient, unit_keys, key_inverse_norm, key_norm_gain)
        .astype(jnp.bfloat16)
        .reshape(rows, -1)
    )
    value_gradient = value_gradient_total.astype(jnp.bfloat16).reshape(rows, -1)
    local_query = jnp.sum(normed_query_gradient * unit_queries, axis=(0, 1, 2))
    local_key = jnp.sum(normed_key_gradient * unit_keys, axis=(0, 1))
    summed_query, summed_key = lax.psum((local_query, local_key), ("outer", "ep", "tp"))
    factor = 1.0 / math.sqrt(rows * seq_devices * QUERY_HEADS)
    return (
        query_grad,
        raw_key_gradient,
        value_gradient,
        summed_query * factor,
        summed_key * factor,
    )


def solution(mesh):
    return jax.shard_map(
        per_device,
        mesh=mesh,
        in_specs=(
            P(("outer", "ep"), "tp"),
            P(("outer", "ep"), "tp"),
            P(("outer", "ep"), "tp"),
            P(("outer", "ep"), "tp"),
            P(("outer", "ep")),
            P(),
            P(),
        ),
        out_specs=(
            P(("outer", "ep"), "tp"),
            P(("outer", "ep"), "tp"),
            P(("outer", "ep"), "tp"),
            P(),
            P(),
        ),
        check_vma=False,
    )
```

profile of v0, /device:TPU:8, one launch (start us, length us, event | category | flops | bytes accessed | tf_op | source)
XLA Modules:
  0.0 278.0 jit_solution(14792579086253987040)
XLA Ops:
  0.6 0.7 fusion.271
  1.3 4.7 %collective-permute-start.4 = (bf16[128]{0:T(256)(128)(2,1)S(1)}, bf16[128]{0:T(256)(128)(2,1)S(1)}, u32[]{:S(2)}, u32[]{:S(2)}) collective-permute-start(bf16[128]{0:T(256)(128)(2,1)S(1)} %get-tuple-element.32), channel_id=1, source_target_pairs={{0,12},{4,16},{8,20},{12,24},{16,28},{20,32},{24,36},{28,40},{32,4... | collective-permute-start | bytes 776 | tf_op jit(solution)/shard_map/ppermute | solution.py:19
  6.0 1.9 collective-permute-start.6
  7.9 2.7 collective-permute-start.8
  10.6 6.8 %collective-permute-start.10 = (bf16[128]{0:T(256)(128)(2,1)S(1)}, bf16[128]{0:T(256)(128)(2,1)S(1)}, u32[]{:S(2)}, u32[]{:S(2)}) collective-permute-start(bf16[128]{0:T(256)(128)(2,1)S(1)} %get-tuple-element.32), channel_id=1, source_target_pairs={{0,24},{4,28},{8,32},{12,36},{16,40},{20,44},{24,48},{28,52},{32,5... | collective-permute-start | bytes 776 | tf_op jit(solution)/shard_map/ppermute | solution.py:19
  17.4 4.6 %collective-permute-start.12 = (bf16[128]{0:T(256)(128)(2,1)S(1)}, bf16[128]{0:T(256)(128)(2,1)S(1)}, u32[]{:S(2)}, u32[]{:S(2)}) collective-permute-start(bf16[128]{0:T(256)(128)(2,1)S(1)} %get-tuple-element.32), channel_id=1, source_target_pairs={{0,28},{4,32},{8,36},{12,40},{16,44},{20,48},{24,52},{28,56},{32,6... | collective-permute-start | bytes 776 | tf_op jit(solution)/shard_map/ppermute | solution.py:19
  22.2 1.2 copy.12
  24.7 0.9 copy-done.1
  25.7 0.5 copy-done.9
  26.3 0.7 copy-done.8
  27.1 2.2 copy.23
  29.3 4.6 %collective-permute-start.13 = (bf16[128,1,128]{2,0,1:T(8,128)(2,1)S(1)}, bf16[128,1,128]{2,0,1:T(8,128)(2,1)S(1)}, u32[]{:S(2)}, u32[]{:S(2)}) collective-permute-start(bf16[128,1,128]{2,0,1:T(8,128)(2,1)S(1)} %fusion.233), channel_id=1, source_target_pairs={{0,28},{4,32},{8,36},{12,40},{16,44},{20,48},{24,52},{28,56},{32,6... | collective-permute-start | bytes 98312 | tf_op jit(solution)/shard_map/ppermute | solution.py:19
  33.9 4.5 %collective-permute-start.11 = (bf16[128,1,128]{2,0,1:T(8,128)(2,1)S(1)}, bf16[128,1,128]{2,0,1:T(8,128)(2,1)S(1)}, u32[]{:S(2)}, u32[]{:S(2)}) collective-permute-start(bf16[128,1,128]{2,0,1:T(8,128)(2,1)S(1)} %fusion.233), channel_id=1, source_target_pairs={{0,24},{4,28},{8,32},{12,36},{16,40},{20,44},{24,48},{28,52},{32,5... | collective-permute-start | bytes 98312 | tf_op jit(solution)/shard_map/ppermute | solution.py:19
  38.5 5.7 %collective-permute-start.9 = (bf16[128,1,128]{2,0,1:T(8,128)(2,1)S(1)}, bf16[128,1,128]{2,0,1:T(8,128)(2,1)S(1)}, u32[]{:S(2)}, u32[]{:S(2)}) collective-permute-start(bf16[128,1,128]{2,0,1:T(8,128)(2,1)S(1)} %fusion.233), channel_id=1, source_target_pairs={{0,20},{4,24},{8,28},{12,32},{16,36},{20,40},{24,44},{28,48},{32,5... | collective-permute-start | bytes 98312 | tf_op jit(solution)/shard_map/ppermute | solution.py:19
  44.3 1.9 collective-permute-start
  46.2 4.6 %collective-permute-start.2 = (bf16[128]{0:T(256)(128)(2,1)S(1)}, bf16[128]{0:T(256)(128)(2,1)S(1)}, u32[]{:S(2)}, u32[]{:S(2)}) collective-permute-start(bf16[128]{0:T(256)(128)(2,1)S(1)} %get-tuple-element.32), channel_id=1, source_target_pairs={{0,8},{4,12},{8,16},{12,20},{16,24},{20,28},{24,32},{28,36},{32,40... | collective-permute-start | bytes 776 | tf_op jit(solution)/shard_map/ppermute | solution.py:19
  51.6 1.8 collective-permute-done
  53.3 2.2 collective-permute-start.7
  55.6 2.9 %collective-permute-start.5 = (bf16[128,1,128]{2,0,1:T(8,128)(2,1)S(1)}, bf16[128,1,128]{2,0,1:T(8,128)(2,1)S(1)}, u32[]{:S(2)}, u32[]{:S(2)}) collective-permute-start(bf16[128,1,128]{2,0,1:T(8,128)(2,1)S(1)} %fusion.233), channel_id=1, source_target_pairs={{0,12},{4,16},{8,20},{12,24},{16,28},{20,32},{24,36},{28,40},{32,4... | collective-permute-start | bytes 98312 | tf_op jit(solution)/shard_map/ppermute | solution.py:19
  58.7 3.6 %collective-permute-start.3 = (bf16[128,1,128]{2,0,1:T(8,128)(2,1)S(1)}, bf16[128,1,128]{2,0,1:T(8,128)(2,1)S(1)}, u32[]{:S(2)}, u32[]{:S(2)}) collective-permute-start(bf16[128,1,128]{2,0,1:T(8,128)(2,1)S(1)} %fusion.233), channel_id=1, source_target_pairs={{0,8},{4,12},{8,16},{12,20},{16,24},{20,28},{24,32},{28,36},{32,40... | collective-permute-start | bytes 98312 | tf_op jit(solution)/shard_map/ppermute | solution.py:19
  62.6 1.9 collective-permute-start.1
  64.9 5.2 %collective-permute-start.14 = (bf16[128,1,128]{0,2,1:T(8,128)(2,1)S(1)}, bf16[128,1,128]{0,2,1:T(8,128)(2,1)S(1)}, u32[]{:S(2)}, u32[]{:S(2)}) collective-permute-start(bf16[128,1,128]{0,2,1:T(8,128)(2,1)S(1)} %bitcast.739), channel_id=1, source_target_pairs={{0,4},{4,8},{8,12},{12,16},{16,20},{20,24},{24,28},{28,32},{32,36}... | collective-permute-start | bytes 98312 | tf_op jit(solution)/shard_map/ppermute | solution.py:19
  70.4 3.2 %collective-permute-start.16 = (bf16[128,1,128]{0,2,1:T(8,128)(2,1)S(1)}, bf16[128,1,128]{0,2,1:T(8,128)(2,1)S(1)}, u32[]{:S(2)}, u32[]{:S(2)}) collective-permute-start(bf16[128,1,128]{0,2,1:T(8,128)(2,1)S(1)} %bitcast.740), channel_id=1, source_target_pairs={{0,12},{4,16},{8,20},{12,24},{16,28},{20,32},{24,36},{28,40},{32,4... | collective-permute-start | bytes 98312 | tf_op jit(solution)/shard_map/ppermute | solution.py:19
  74.0 1.9 collective-permute-start.17
  76.2 3.3 %collective-permute-start.18 = (bf16[128,1,128]{0,2,1:T(8,128)(2,1)S(1)}, bf16[128,1,128]{0,2,1:T(8,128)(2,1)S(1)}, u32[]{:S(2)}, u32[]{:S(2)}) collective-permute-start(bf16[128,1,128]{0,2,1:T(8,128)(2,1)S(1)} %bitcast.742), channel_id=1, source_target_pairs={{0,20},{4,24},{8,28},{12,32},{16,36},{20,40},{24,44},{28,48},{32,5... | collective-permute-start | bytes 98312 | tf_op jit(solution)/shard_map/ppermute | solution.py:19
  79.9 5.7 %collective-permute-start.19 = (bf16[128,1,128]{0,2,1:T(8,128)(2,1)S(1)}, bf16[128,1,128]{0,2,1:T(8,128)(2,1)S(1)}, u32[]{:S(2)}, u32[]{:S(2)}) collective-permute-start(bf16[128,1,128]{0,2,1:T(8,128)(2,1)S(1)} %bitcast.743), channel_id=1, source_target_pairs={{0,24},{4,28},{8,32},{12,36},{16,40},{20,44},{24,48},{28,52},{32,5... | collective-permute-start | bytes 98312 | tf_op jit(solution)/shard_map/ppermute | solution.py:19
  85.9 2.4 fusion.103
  88.6 4.0 %collective-permute-start.20 = (bf16[128,1,128]{0,2,1:T(8,128)(2,1)S(1)}, bf16[128,1,128]{0,2,1:T(8,128)(2,1)S(1)}, u32[]{:S(2)}, u32[]{:S(2)}) collective-permute-start(bf16[128,1,128]{0,2,1:T(8,128)(2,1)S(1)} %bitcast.744), channel_id=1, source_target_pairs={{0,28},{4,32},{8,36},{12,40},{16,44},{20,48},{24,52},{28,56},{32,6... | collective-permute-start | bytes 98312 | tf_op jit(solution)/shard_map/ppermute | solution.py:19
  93.0 0.9 fusion.90
  93.9 4.1 %collective-permute-start.15 = (bf16[128,1,128]{0,2,1:T(8,128)(2,1)S(1)}, bf16[128,1,128]{0,2,1:T(8,128)(2,1)S(1)}, u32[]{:S(2)}, u32[]{:S(2)}) collective-permute-start(bf16[128,1,128]{0,2,1:T(8,128)(2,1)S(1)} %bitcast.745), channel_id=1, source_target_pairs={{0,8},{4,12},{8,16},{12,20},{16,24},{20,28},{24,32},{28,36},{32,40... | collective-permute-start | bytes 98312 | tf_op jit(solution)/shard_map/ppermute | solution.py:19
  98.3 0.9 fusion.89
  100.3 1.0 fusion.87
  101.6 1.0 fusion.86
  102.9 0.9 fusion.92
  104.1 0.6 fusion.54
  105.1 0.4 fusion.57
  105.8 6.2 %collective-permute-start.22 = (bf16[128,1,128]{2,0,1:T(8,128)(2,1)S(1)}, bf16[128,1,128]{2,0,1:T(8,128)(2,1)S(1)}, u32[]{:S(2)}, u32[]{:S(2)}) collective-permute-start(bf16[128,1,128]{2,0,1:T(8,128)(2,1)S(1)} %fusion.98), channel_id=1, source_target_pairs={{8,0},{12,4},{16,8},{20,12},{24,16},{28,20},{32,24},{36,28},{40,32... | collective-permute-start | bytes 98312 | tf_op jit(solution)/shard_map/ppermute | solution.py:19
  112.0 0.4 fusion.56
  112.7 2.2 collective-permute-start.21
  114.9 0.4 fusion.58
  115.6 3.2 %collective-permute-start.23 = (bf16[128,1,128]{2,0,1:T(8,128)(2,1)S(1)}, bf16[128,1,128]{2,0,1:T(8,128)(2,1)S(1)}, u32[]{:S(2)}, u32[]{:S(2)}) collective-permute-start(bf16[128,1,128]{2,0,1:T(8,128)(2,1)S(1)} %fusion.97), channel_id=1, source_target_pairs={{12,0},{16,4},{20,8},{24,12},{28,16},{32,20},{36,24},{40,28},{44,3... | collective-permute-start | bytes 98312 | tf_op jit(solution)/shard_map/ppermute | solution.py:19
  118.9 0.4 fusion.59
  119.6 2.5 collective-permute-start.24
  122.8 3.0 %collective-permute-start.25 = (bf16[128,1,128]{2,0,1:T(8,128)(2,1)S(1)}, bf16[128,1,128]{2,0,1:T(8,128)(2,1)S(1)}, u32[]{:S(2)}, u32[]{:S(2)}) collective-permute-start(bf16[128,1,128]{2,0,1:T(8,128)(2,1)S(1)} %fusion.95), channel_id=1, source_target_pairs={{20,0},{24,4},{28,8},{32,12},{36,16},{40,20},{44,24},{48,28},{52,3... | collective-permute-start | bytes 98312 | tf_op jit(solution)/shard_map/ppermute | solution.py:19
  126.6 0.4 fusion.230
  129.3 1.0 multiply_reduce_fusion
  130.3 1.1 multiply_convert_fusion.1
  131.7 3.5 %collective-permute-start.26 = (bf16[128,1,128]{2,0,1:T(8,128)(2,1)S(1)}, bf16[128,1,128]{2,0,1:T(8,128)(2,1)S(1)}, u32[]{:S(2)}, u32[]{:S(2)}) collective-permute-start(bf16[128,1,128]{2,0,1:T(8,128)(2,1)S(1)} %fusion.94), channel_id=1, source_target_pairs={{24,0},{28,4},{32,8},{36,12},{40,16},{44,20},{48,24},{52,28},{56,3... | collective-permute-start | bytes 98312 | tf_op jit(solution)/shard_map/ppermute | solution.py:19
  135.2 1.9 collective-permute-start.27
  137.5 1.0 copy.89
  138.5 3.5 %collective-permute-start.30 = (bf16[128,1,128]{2,0,1:T(8,128)(2,1)S(1)}, bf16[128,1,128]{2,0,1:T(8,128)(2,1)S(1)}, u32[]{:S(2)}, u32[]{:S(2)}) collective-permute-start(bf16[128,1,128]{2,0,1:T(8,128)(2,1)S(1)} %copy-done.14), channel_id=1, source_target_pairs={{12,0},{16,4},{20,8},{24,12},{28,16},{32,20},{36,24},{40,28},{44,3... | collective-permute-start | bytes 98312 | tf_op jit(solution)/shard_map/ppermute | solution.py:19
  142.1 3.3 %collective-permute-start.31 = (bf16[128,1,128]{2,0,1:T(8,128)(2,1)S(1)}, bf16[128,1,128]{2,0,1:T(8,128)(2,1)S(1)}, u32[]{:S(2)}, u32[]{:S(2)}) collective-permute-start(bf16[128,1,128]{2,0,1:T(8,128)(2,1)S(1)} %copy-done.15), channel_id=1, source_target_pairs={{16,0},{20,4},{24,8},{28,12},{32,16},{36,20},{40,24},{44,28},{48,3... | collective-permute-start | bytes 98312 | tf_op jit(solution)/shard_map/ppermute | solution.py:19
  145.4 3.3 %collective-permute-start.32 = (bf16[128,1,128]{2,0,1:T(8,128)(2,1)S(1)}, bf16[128,1,128]{2,0,1:T(8,128)(2,1)S(1)}, u32[]{:S(2)}, u32[]{:S(2)}) collective-permute-start(bf16[128,1,128]{2,0,1:T(8,128)(2,1)S(1)} %fusion.88), channel_id=1, source_target_pairs={{20,0},{24,4},{28,8},{32,12},{36,16},{40,20},{44,24},{48,28},{52,3... | collective-permute-start | bytes 98312 | tf_op jit(solution)/shard_map/ppermute | solution.py:19
  148.7 2.8 %collective-permute-start.33 = (bf16[128,1,128]{2,0,1:T(8,128)(2,1)S(1)}, bf16[128,1,128]{2,0,1:T(8,128)(2,1)S(1)}, u32[]{:S(2)}, u32[]{:S(2)}) collective-permute-start(bf16[128,1,128]{2,0,1:T(8,128)(2,1)S(1)} %copy-done.11), channel_id=1, source_target_pairs={{24,0},{28,4},{32,8},{36,12},{40,16},{44,20},{48,24},{52,28},{56,3... | collective-permute-start | bytes 98312 | tf_op jit(solution)/shard_map/ppermute | solution.py:19
  151.6 1.9 collective-permute-start.34
  153.5 0.4 fusion.185
  153.9 107.3 %all-reduce = (f32[128]{0:T(128)S(1)}, f32[128]{0:T(128)S(1)}) all-reduce(f32[128]{0:T(128)S(1)} %get-tuple-element.10, f32[128]{0:T(128)S(1)} %get-tuple-element.12), channel_id=1, replica_groups=mesh['outer'=48,'ep'=4,'tp'=4] {'outer','ep','tp'}, use_global_device_ids=true, to_apply=%region_22.23 | all-reduce | flops 256 | bytes 2048 | tf_op jit(solution)/shard_map/psum | solution.py:159
  261.2 0.7 fusion.193
  261.9 0.5 broadcast_multiply_fusion.1
  262.5 7.2 %collective-permute-start.28 = (bf16[128,1,128]{2,0,1:T(8,128)(2,1)S(1)}, bf16[128,1,128]{2,0,1:T(8,128)(2,1)S(1)}, u32[]{:S(2)}, u32[]{:S(2)}) collective-permute-start(bf16[128,1,128]{2,0,1:T(8,128)(2,1)S(1)} %copy-done.13), channel_id=1, source_target_pairs={{4,0},{8,4},{12,8},{16,12},{20,16},{24,20},{28,24},{32,28},{36,32}... | collective-permute-start | bytes 98312 | tf_op jit(solution)/shard_map/ppermute | solution.py:19
  269.7 3.7 %collective-permute-start.29 = (bf16[128,1,128]{2,0,1:T(8,128)(2,1)S(1)}, bf16[128,1,128]{2,0,1:T(8,128)(2,1)S(1)}, u32[]{:S(2)}, u32[]{:S(2)}) collective-permute-start(bf16[128,1,128]{2,0,1:T(8,128)(2,1)S(1)} %fusion.91), channel_id=1, source_target_pairs={{8,0},{12,4},{16,8},{20,12},{24,16},{28,20},{32,24},{36,28},{40,32... | collective-permute-start | bytes 98312 | tf_op jit(solution)/shard_map/ppermute | solution.py:19
  273.4 0.5 broadcast_multiply_fusion.2
  273.9 3.1 %collective-permute-done.29 = bf16[128,1,128]{2,0,1:T(8,128)(2,1)S(1)} collective-permute-done((bf16[128,1,128]{2,0,1:T(8,128)(2,1)S(1)}, bf16[128,1,128]{2,0,1:T(8,128)(2,1)S(1)}, u32[]{:S(2)}, u32[]{:S(2)}) %collective-permute-start.29) | collective-permute-done | bytes 32800 | tf_op jit(solution)/shard_map/ppermute | solution.py:19
  277.0 1.0 fusion.192
  (129 shorter events, 13.8 us)
Async XLA Ops:
  1.3 28.0 %collective-permute-start.4 = (bf16[128]{0:T(256)(128)(2,1)S(1)}, bf16[128]{0:T(256)(128)(2,1)S(1)}, u32[]{:S(2)}, u32[]{:S(2)}) collective-permute-start(bf16[128]{0:T(256)(128)(2,1)S(1)} %get-tuple-element.32), channel_id=1, source_target_pairs={{0,12},{4,16},{8,20},{12,24},{16,28},{20,32},{24,36},{28,40},{32,4... | collective-permute-start | bytes 776 | tf_op jit(solution)/shard_map/ppermute | solution.py:19
  6.0 28.0 %collective-permute-start.6 = (bf16[128]{0:T(256)(128)(2,1)S(1)}, bf16[128]{0:T(256)(128)(2,1)S(1)}, u32[]{:S(2)}, u32[]{:S(2)}) collective-permute-start(bf16[128]{0:T(256)(128)(2,1)S(1)} %get-tuple-element.32), channel_id=1, source_target_pairs={{0,16},{4,20},{8,24},{12,28},{16,32},{20,36},{24,40},{28,44},{32,4... | collective-permute-start | bytes 776 | tf_op jit(solution)/shard_map/ppermute | solution.py:19
  7.9 30.6 %collective-permute-start.8 = (bf16[128]{0:T(256)(128)(2,1)S(1)}, bf16[128]{0:T(256)(128)(2,1)S(1)}, u32[]{:S(2)}, u32[]{:S(2)}) collective-permute-start(bf16[128]{0:T(256)(128)(2,1)S(1)} %get-tuple-element.32), channel_id=1, source_target_pairs={{0,20},{4,24},{8,28},{12,32},{16,36},{20,40},{24,44},{28,48},{32,5... | collective-permute-start | bytes 776 | tf_op jit(solution)/shard_map/ppermute | solution.py:19
  10.6 33.6 %collective-permute-start.10 = (bf16[128]{0:T(256)(128)(2,1)S(1)}, bf16[128]{0:T(256)(128)(2,1)S(1)}, u32[]{:S(2)}, u32[]{:S(2)}) collective-permute-start(bf16[128]{0:T(256)(128)(2,1)S(1)} %get-tuple-element.32), channel_id=1, source_target_pairs={{0,24},{4,28},{8,32},{12,36},{16,40},{20,44},{24,48},{28,52},{32,5... | collective-permute-start | bytes 776 | tf_op jit(solution)/shard_map/ppermute | solution.py:19
  17.4 28.8 %collective-permute-start.12 = (bf16[128]{0:T(256)(128)(2,1)S(1)}, bf16[128]{0:T(256)(128)(2,1)S(1)}, u32[]{:S(2)}, u32[]{:S(2)}) collective-permute-start(bf16[128]{0:T(256)(128)(2,1)S(1)} %get-tuple-element.32), channel_id=1, source_target_pairs={{0,28},{4,32},{8,36},{12,40},{16,44},{20,48},{24,52},{28,56},{32,6... | collective-permute-start | bytes 776 | tf_op jit(solution)/shard_map/ppermute | solution.py:19
  23.6 0.7 copy-start.10
  23.6 0.8 copy-start.5
  24.5 1.1 copy-start.1
  25.6 0.7 copy-start.9
  26.2 0.8 copy-start.8
  29.3 29.4 %collective-permute-start.13 = (bf16[128,1,128]{2,0,1:T(8,128)(2,1)S(1)}, bf16[128,1,128]{2,0,1:T(8,128)(2,1)S(1)}, u32[]{:S(2)}, u32[]{:S(2)}) collective-permute-start(bf16[128,1,128]{2,0,1:T(8,128)(2,1)S(1)} %fusion.233), channel_id=1, source_target_pairs={{0,28},{4,32},{8,36},{12,40},{16,44},{20,48},{24,52},{28,56},{32,6... | collective-permute-start | bytes 98312 | tf_op jit(solution)/shard_map/ppermute | solution.py:19
  33.9 28.7 %collective-permute-start.11 = (bf16[128,1,128]{2,0,1:T(8,128)(2,1)S(1)}, bf16[128,1,128]{2,0,1:T(8,128)(2,1)S(1)}, u32[]{:S(2)}, u32[]{:S(2)}) collective-permute-start(bf16[128,1,128]{2,0,1:T(8,128)(2,1)S(1)} %fusion.233), channel_id=1, source_target_pairs={{0,24},{4,28},{8,32},{12,36},{16,40},{20,44},{24,48},{28,52},{32,5... | collective-permute-start | bytes 98312 | tf_op jit(solution)/shard_map/ppermute | solution.py:19
  38.5 26.4 %collective-permute-start.9 = (bf16[128,1,128]{2,0,1:T(8,128)(2,1)S(1)}, bf16[128,1,128]{2,0,1:T(8,128)(2,1)S(1)}, u32[]{:S(2)}, u32[]{:S(2)}) collective-permute-start(bf16[128,1,128]{2,0,1:T(8,128)(2,1)S(1)} %fusion.233), channel_id=1, source_target_pairs={{0,20},{4,24},{8,28},{12,32},{16,36},{20,40},{24,44},{28,48},{32,5... | collective-permute-start | bytes 98312 | tf_op jit(solution)/shard_map/ppermute | solution.py:19
  44.3 9.1 %collective-permute-start = (bf16[128]{0:T(256)(128)(2,1)S(1)}, bf16[128]{0:T(256)(128)(2,1)S(1)}, u32[]{:S(2)}, u32[]{:S(2)}) collective-permute-start(bf16[128]{0:T(256)(128)(2,1)S(1)} %get-tuple-element.32), channel_id=1, source_target_pairs={{0,4},{4,8},{8,12},{12,16},{16,20},{20,24},{24,28},{28,32},{32,36}... | collective-permute-start | bytes 776 | tf_op jit(solution)/shard_map/ppermute | solution.py:19
  46.2 9.4 %collective-permute-start.2 = (bf16[128]{0:T(256)(128)(2,1)S(1)}, bf16[128]{0:T(256)(128)(2,1)S(1)}, u32[]{:S(2)}, u32[]{:S(2)}) collective-permute-start(bf16[128]{0:T(256)(128)(2,1)S(1)} %get-tuple-element.32), channel_id=1, source_target_pairs={{0,8},{4,12},{8,16},{12,20},{16,24},{20,28},{24,32},{28,36},{32,40... | collective-permute-start | bytes 776 | tf_op jit(solution)/shard_map/ppermute | solution.py:19
  53.3 17.1 %collective-permute-start.7 = (bf16[128,1,128]{2,0,1:T(8,128)(2,1)S(1)}, bf16[128,1,128]{2,0,1:T(8,128)(2,1)S(1)}, u32[]{:S(2)}, u32[]{:S(2)}) collective-permute-start(bf16[128,1,128]{2,0,1:T(8,128)(2,1)S(1)} %fusion.233), channel_id=1, source_target_pairs={{0,16},{4,20},{8,24},{12,28},{16,32},{20,36},{24,40},{28,44},{32,4... | collective-permute-start | bytes 98312 | tf_op jit(solution)/shard_map/ppermute | solution.py:19
  55.6 18.4 %collective-permute-start.5 = (bf16[128,1,128]{2,0,1:T(8,128)(2,1)S(1)}, bf16[128,1,128]{2,0,1:T(8,128)(2,1)S(1)}, u32[]{:S(2)}, u32[]{:S(2)}) collective-permute-start(bf16[128,1,128]{2,0,1:T(8,128)(2,1)S(1)} %fusion.233), channel_id=1, source_target_pairs={{0,12},{4,16},{8,20},{12,24},{16,28},{20,32},{24,36},{28,40},{32,4... | collective-permute-start | bytes 98312 | tf_op jit(solution)/shard_map/ppermute | solution.py:19
  58.7 17.5 %collective-permute-start.3 = (bf16[128,1,128]{2,0,1:T(8,128)(2,1)S(1)}, bf16[128,1,128]{2,0,1:T(8,128)(2,1)S(1)}, u32[]{:S(2)}, u32[]{:S(2)}) collective-permute-start(bf16[128,1,128]{2,0,1:T(8,128)(2,1)S(1)} %fusion.233), channel_id=1, source_target_pairs={{0,8},{4,12},{8,16},{12,20},{16,24},{20,28},{24,32},{28,36},{32,40... | collective-permute-start | bytes 98312 | tf_op jit(solution)/shard_map/ppermute | solution.py:19
  62.6 17.2 %collective-permute-start.1 = (bf16[128,1,128]{2,0,1:T(8,128)(2,1)S(1)}, bf16[128,1,128]{2,0,1:T(8,128)(2,1)S(1)}, u32[]{:S(2)}, u32[]{:S(2)}) collective-permute-start(bf16[128,1,128]{2,0,1:T(8,128)(2,1)S(1)} %fusion.233), channel_id=1, source_target_pairs={{0,4},{4,8},{8,12},{12,16},{16,20},{20,24},{24,28},{28,32},{32,36}... | collective-permute-start | bytes 98312 | tf_op jit(solution)/shard_map/ppermute | solution.py:19
  64.9 37.7 %collective-permute-start.14 = (bf16[128,1,128]{0,2,1:T(8,128)(2,1)S(1)}, bf16[128,1,128]{0,2,1:T(8,128)(2,1)S(1)}, u32[]{:S(2)}, u32[]{:S(2)}) collective-permute-start(bf16[128,1,128]{0,2,1:T(8,128)(2,1)S(1)} %bitcast.739), channel_id=1, source_target_pairs={{0,4},{4,8},{8,12},{12,16},{16,20},{20,24},{24,28},{28,32},{32,36}... | collective-permute-start | bytes 98312 | tf_op jit(solution)/shard_map/ppermute | solution.py:19
  70.4 18.2 %collective-permute-start.16 = (bf16[128,1,128]{0,2,1:T(8,128)(2,1)S(1)}, bf16[128,1,128]{0,2,1:T(8,128)(2,1)S(1)}, u32[]{:S(2)}, u32[]{:S(2)}) collective-permute-start(bf16[128,1,128]{0,2,1:T(8,128)(2,1)S(1)} %bitcast.740), channel_id=1, source_target_pairs={{0,12},{4,16},{8,20},{12,24},{16,28},{20,32},{24,36},{28,40},{32,4... | collective-permute-start | bytes 98312 | tf_op jit(solution)/shard_map/ppermute | solution.py:19
  74.0 19.9 %collective-permute-start.17 = (bf16[128,1,128]{0,2,1:T(8,128)(2,1)S(1)}, bf16[128,1,128]{0,2,1:T(8,128)(2,1)S(1)}, u32[]{:S(2)}, u32[]{:S(2)}) collective-permute-start(bf16[128,1,128]{0,2,1:T(8,128)(2,1)S(1)} %bitcast.741), channel_id=1, source_target_pairs={{0,16},{4,20},{8,24},{12,28},{16,32},{20,36},{24,40},{28,44},{32,4... | collective-permute-start | bytes 98312 | tf_op jit(solution)/shard_map/ppermute | solution.py:19
  76.2 23.0 %collective-permute-start.18 = (bf16[128,1,128]{0,2,1:T(8,128)(2,1)S(1)}, bf16[128,1,128]{0,2,1:T(8,128)(2,1)S(1)}, u32[]{:S(2)}, u32[]{:S(2)}) collective-permute-start(bf16[128,1,128]{0,2,1:T(8,128)(2,1)S(1)} %bitcast.742), channel_id=1, source_target_pairs={{0,20},{4,24},{8,28},{12,32},{16,36},{20,40},{24,44},{28,48},{32,5... | collective-permute-start | bytes 98312 | tf_op jit(solution)/shard_map/ppermute | solution.py:19
  79.9 20.1 %collective-permute-start.19 = (bf16[128,1,128]{0,2,1:T(8,128)(2,1)S(1)}, bf16[128,1,128]{0,2,1:T(8,128)(2,1)S(1)}, u32[]{:S(2)}, u32[]{:S(2)}) collective-permute-start(bf16[128,1,128]{0,2,1:T(8,128)(2,1)S(1)} %bitcast.743), channel_id=1, source_target_pairs={{0,24},{4,28},{8,32},{12,36},{16,40},{20,44},{24,48},{28,52},{32,5... | collective-permute-start | bytes 98312 | tf_op jit(solution)/shard_map/ppermute | solution.py:19
  88.6 4.4 %copy-start.6 = (bf16[128,2048]{1,0:T(8,128)(2,1)S(1)}, bf16[128,2048]{1,0:T(8,128)(2,1)}, u32[]{:S(2)}) copy-start(bf16[128,2048]{1,0:T(8,128)(2,1)} %param.10) | copy-start | bytes 1572868
  88.6 12.6 %collective-permute-start.20 = (bf16[128,1,128]{0,2,1:T(8,128)(2,1)S(1)}, bf16[128,1,128]{0,2,1:T(8,128)(2,1)S(1)}, u32[]{:S(2)}, u32[]{:S(2)}) collective-permute-start(bf16[128,1,128]{0,2,1:T(8,128)(2,1)S(1)} %bitcast.744), channel_id=1, source_target_pairs={{0,28},{4,32},{8,36},{12,40},{16,44},{20,48},{24,52},{28,56},{32,6... | collective-permute-start | bytes 98312 | tf_op jit(solution)/shard_map/ppermute | solution.py:19
  93.9 9.9 %collective-permute-start.15 = (bf16[128,1,128]{0,2,1:T(8,128)(2,1)S(1)}, bf16[128,1,128]{0,2,1:T(8,128)(2,1)S(1)}, u32[]{:S(2)}, u32[]{:S(2)}) collective-permute-start(bf16[128,1,128]{0,2,1:T(8,128)(2,1)S(1)} %bitcast.745), channel_id=1, source_target_pairs={{0,8},{4,12},{8,16},{12,20},{16,24},{20,28},{24,32},{28,36},{32,40... | collective-permute-start | bytes 98312 | tf_op jit(solution)/shard_map/ppermute | solution.py:19
  102.9 1.2 copy-start
  105.1 21.4 %copy-start.2 = (bf16[16,128,128]{1,2,0:T(8,128)(2,1)}, bf16[16,128,128]{1,2,0:T(8,128)(2,1)S(1)}, u32[]{:S(2)}) copy-start(bf16[16,128,128]{1,2,0:T(8,128)(2,1)S(1)} %fusion.55) | copy-start | bytes 1572868
  105.8 25.9 %collective-permute-start.22 = (bf16[128,1,128]{2,0,1:T(8,128)(2,1)S(1)}, bf16[128,1,128]{2,0,1:T(8,128)(2,1)S(1)}, u32[]{:S(2)}, u32[]{:S(2)}) collective-permute-start(bf16[128,1,128]{2,0,1:T(8,128)(2,1)S(1)} %fusion.98), channel_id=1, source_target_pairs={{8,0},{12,4},{16,8},{20,12},{24,16},{28,20},{32,24},{36,28},{40,32... | collective-permute-start | bytes 98312 | tf_op jit(solution)/shard_map/ppermute | solution.py:19
  112.7 22.5 %collective-permute-start.21 = (bf16[128,1,128]{2,0,1:T(8,128)(2,1)S(1)}, bf16[128,1,128]{2,0,1:T(8,128)(2,1)S(1)}, u32[]{:S(2)}, u32[]{:S(2)}) collective-permute-start(bf16[128,1,128]{2,0,1:T(8,128)(2,1)S(1)} %fusion.99), channel_id=1, source_target_pairs={{4,0},{8,4},{12,8},{16,12},{20,16},{24,20},{28,24},{32,28},{36,32}... | collective-permute-start | bytes 98312 | tf_op jit(solution)/shard_map/ppermute | solution.py:19
  115.6 22.9 %collective-permute-start.23 = (bf16[128,1,128]{2,0,1:T(8,128)(2,1)S(1)}, bf16[128,1,128]{2,0,1:T(8,128)(2,1)S(1)}, u32[]{:S(2)}, u32[]{:S(2)}) collective-permute-start(bf16[128,1,128]{2,0,1:T(8,128)(2,1)S(1)} %fusion.97), channel_id=1, source_target_pairs={{12,0},{16,4},{20,8},{24,12},{28,16},{32,20},{36,24},{40,28},{44,3... | collective-permute-start | bytes 98312 | tf_op jit(solution)/shard_map/ppermute | solution.py:19
  119.6 22.5 %collective-permute-start.24 = (bf16[128,1,128]{2,0,1:T(8,128)(2,1)S(1)}, bf16[128,1,128]{2,0,1:T(8,128)(2,1)S(1)}, u32[]{:S(2)}, u32[]{:S(2)}) collective-permute-start(bf16[128,1,128]{2,0,1:T(8,128)(2,1)S(1)} %fusion.96), channel_id=1, source_target_pairs={{16,0},{20,4},{24,8},{28,12},{32,16},{36,20},{40,24},{44,28},{48,3... | collective-permute-start | bytes 98312 | tf_op jit(solution)/shard_map/ppermute | solution.py:19
  122.8 22.6 %collective-permute-start.25 = (bf16[128,1,128]{2,0,1:T(8,128)(2,1)S(1)}, bf16[128,1,128]{2,0,1:T(8,128)(2,1)S(1)}, u32[]{:S(2)}, u32[]{:S(2)}) collective-permute-start(bf16[128,1,128]{2,0,1:T(8,128)(2,1)S(1)} %fusion.95), channel_id=1, source_target_pairs={{20,0},{24,4},{28,8},{32,12},{36,16},{40,20},{44,24},{48,28},{52,3... | collective-permute-start | bytes 98312 | tf_op jit(solution)/shard_map/ppermute | solution.py:19
  131.7 5.8 %copy-start.4 = (bf16[128,1,16,128]{0,3,2,1:T(8,128)(2,1)S(1)}, bf16[128,1,16,128]{0,3,2,1:T(8,128)(2,1)}, u32[]{:S(2)}) copy-start(bf16[128,1,16,128]{0,3,2,1:T(8,128)(2,1)} %multiply_convert_fusion.1) | copy-start | bytes 1572868
  131.7 17.0 %collective-permute-start.26 = (bf16[128,1,128]{2,0,1:T(8,128)(2,1)S(1)}, bf16[128,1,128]{2,0,1:T(8,128)(2,1)S(1)}, u32[]{:S(2)}, u32[]{:S(2)}) collective-permute-start(bf16[128,1,128]{2,0,1:T(8,128)(2,1)S(1)} %fusion.94), channel_id=1, source_target_pairs={{24,0},{28,4},{32,8},{36,12},{40,16},{44,20},{48,24},{52,28},{56,3... | collective-permute-start | bytes 98312 | tf_op jit(solution)/shard_map/ppermute | solution.py:19
  135.2 16.4 %collective-permute-start.27 = (bf16[128,1,128]{2,0,1:T(8,128)(2,1)S(1)}, bf16[128,1,128]{2,0,1:T(8,128)(2,1)S(1)}, u32[]{:S(2)}, u32[]{:S(2)}) collective-permute-start(bf16[128,1,128]{2,0,1:T(8,128)(2,1)S(1)} %fusion.93), channel_id=1, source_target_pairs={{28,0},{32,4},{36,8},{40,12},{44,16},{48,20},{52,24},{56,28},{60,3... | collective-permute-start | bytes 98312 | tf_op jit(solution)/shard_map/ppermute | solution.py:19
  137.5 1.1 copy-start.14
  137.5 4.6 %copy-start.15 = (bf16[128,1,128]{2,0,1:T(8,128)(2,1)S(1)}, bf16[128,1,128]{2,0,1:T(8,128)(2,1)}, u32[]{:S(2)}) copy-start(bf16[128,1,128]{2,0,1:T(8,128)(2,1)} %fusion.89) | copy-start | bytes 98308
  137.5 11.2 %copy-start.11 = (bf16[128,1,128]{2,0,1:T(8,128)(2,1)S(1)}, bf16[128,1,128]{2,0,1:T(8,128)(2,1)}, u32[]{:S(2)}) copy-start(bf16[128,1,128]{2,0,1:T(8,128)(2,1)} %fusion.87) | copy-start | bytes 98308
  137.5 14.1 %copy-start.12 = (bf16[128,1,128]{2,0,1:T(8,128)(2,1)S(1)}, bf16[128,1,128]{2,0,1:T(8,128)(2,1)}, u32[]{:S(2)}) copy-start(bf16[128,1,128]{2,0,1:T(8,128)(2,1)} %fusion.86) | copy-start | bytes 98308
  137.5 16.0 %copy-start.3 = (bf16[16,128,128]{1,2,0:T(8,128)(2,1)S(1)}, bf16[16,128,128]{1,2,0:T(8,128)(2,1)}, u32[]{:S(2)}) copy-start(bf16[16,128,128]{1,2,0:T(8,128)(2,1)} %copy-done.2) | copy-start | bytes 1572868
  138.5 138.5 %copy-start.7 = (bf16[128,2048]{1,0:T(8,128)(2,1)S(1)}, bf16[128,2048]{1,0:T(8,128)(2,1)}, u32[]{:S(2)}) copy-start(bf16[128,2048]{1,0:T(8,128)(2,1)} %param.10) | copy-start | bytes 1572868
  138.5 123.9 %collective-permute-start.30 = (bf16[128,1,128]{2,0,1:T(8,128)(2,1)S(1)}, bf16[128,1,128]{2,0,1:T(8,128)(2,1)S(1)}, u32[]{:S(2)}, u32[]{:S(2)}) collective-permute-start(bf16[128,1,128]{2,0,1:T(8,128)(2,1)S(1)} %copy-done.14), channel_id=1, source_target_pairs={{12,0},{16,4},{20,8},{24,12},{28,16},{32,20},{36,24},{40,28},{44,3... | collective-permute-start | bytes 98312 | tf_op jit(solution)/shard_map/ppermute | solution.py:19
  142.1 127.6 %collective-permute-start.31 = (bf16[128,1,128]{2,0,1:T(8,128)(2,1)S(1)}, bf16[128,1,128]{2,0,1:T(8,128)(2,1)S(1)}, u32[]{:S(2)}, u32[]{:S(2)}) collective-permute-start(bf16[128,1,128]{2,0,1:T(8,128)(2,1)S(1)} %copy-done.15), channel_id=1, source_target_pairs={{16,0},{20,4},{24,8},{28,12},{32,16},{36,20},{40,24},{44,28},{48,3... | collective-permute-start | bytes 98312 | tf_op jit(solution)/shard_map/ppermute | solution.py:19
  145.4 128.5 %collective-permute-start.32 = (bf16[128,1,128]{2,0,1:T(8,128)(2,1)S(1)}, bf16[128,1,128]{2,0,1:T(8,128)(2,1)S(1)}, u32[]{:S(2)}, u32[]{:S(2)}) collective-permute-start(bf16[128,1,128]{2,0,1:T(8,128)(2,1)S(1)} %fusion.88), channel_id=1, source_target_pairs={{20,0},{24,4},{28,8},{32,12},{36,16},{40,20},{44,24},{48,28},{52,3... | collective-permute-start | bytes 98312 | tf_op jit(solution)/shard_map/ppermute | solution.py:19
  148.7 125.2 %collective-permute-start.33 = (bf16[128,1,128]{2,0,1:T(8,128)(2,1)S(1)}, bf16[128,1,128]{2,0,1:T(8,128)(2,1)S(1)}, u32[]{:S(2)}, u32[]{:S(2)}) collective-permute-start(bf16[128,1,128]{2,0,1:T(8,128)(2,1)S(1)} %copy-done.11), channel_id=1, source_target_pairs={{24,0},{28,4},{32,8},{36,12},{40,16},{44,20},{48,24},{52,28},{56,3... | collective-permute-start | bytes 98312 | tf_op jit(solution)/shard_map/ppermute | solution.py:19
  151.6 122.4 %collective-permute-start.34 = (bf16[128,1,128]{2,0,1:T(8,128)(2,1)S(1)}, bf16[128,1,128]{2,0,1:T(8,128)(2,1)S(1)}, u32[]{:S(2)}, u32[]{:S(2)}) collective-permute-start(bf16[128,1,128]{2,0,1:T(8,128)(2,1)S(1)} %copy-done.12), channel_id=1, source_target_pairs={{28,0},{32,4},{36,8},{40,12},{44,16},{48,20},{52,24},{56,28},{60,3... | collective-permute-start | bytes 98312 | tf_op jit(solution)/shard_map/ppermute | solution.py:19
  261.2 1.3 copy-start.13
  262.5 11.5 %collective-permute-start.28 = (bf16[128,1,128]{2,0,1:T(8,128)(2,1)S(1)}, bf16[128,1,128]{2,0,1:T(8,128)(2,1)S(1)}, u32[]{:S(2)}, u32[]{:S(2)}) collective-permute-start(bf16[128,1,128]{2,0,1:T(8,128)(2,1)S(1)} %copy-done.13), channel_id=1, source_target_pairs={{4,0},{8,4},{12,8},{16,12},{20,16},{24,20},{28,24},{32,28},{36,32}... | collective-permute-start | bytes 98312 | tf_op jit(solution)/shard_map/ppermute | solution.py:19
  269.7 7.3 %collective-permute-start.29 = (bf16[128,1,128]{2,0,1:T(8,128)(2,1)S(1)}, bf16[128,1,128]{2,0,1:T(8,128)(2,1)S(1)}, u32[]{:S(2)}, u32[]{:S(2)}) collective-permute-start(bf16[128,1,128]{2,0,1:T(8,128)(2,1)S(1)} %fusion.91), channel_id=1, source_target_pairs={{8,0},{12,4},{16,8},{20,12},{24,16},{28,20},{32,24},{36,28},{40,32... | collective-permute-start | bytes 98312 | tf_op jit(solution)/shard_map/ppermute | solution.py:19
where the time goes:
time: 279 us; the launch traced here: 278 us
  starting transfers between devices  128 us (46%)
  blocking collectives  107 us (38%)
  matrix products  20.8 us (7%)
  local copies, waits for them, and re-layouts  7.74 us (3%)
  other arithmetic  7.15 us (3%)
  waiting for transfers between devices  5.01 us (2%)
    ppermute x35, starting transfers between devices, from_behind(): return lax.ppermute(block, axis, route)  128 us
    psum x1, blocking collectives, per_device(): lax.psum((local_query, local_key), ('outer', 'ep', 'tp'))  107 us
    dot_general x8, matrix products, per_device(): jnp.einsum('hgqk,qhgd->khd', block_probs_b, gradient_list, preferred_elem...  6.36 us
  transfers between devices with their start and end apart: 35, of which 3 were waited for; matrix products, arithmetic and copies ran while one was open for 11% of the time, Pallas kernels for 0%

commit v1 on v0

v1 whole, which is shorter than its diff:
```python
import math

import jax
import jax.numpy as jnp
from jax import lax
from jax.experimental import pallas as pl
from jax.experimental.pallas import tpu as pltpu
from jax.sharding import Mesh
from jax.sharding import PartitionSpec as P

HEAD_SIZE = 128
ROWS = 128
SPAN = 8
HEADS = 16
PAIRS = 2
TOKENS = SPAN * ROWS
EXTRA = 16
CHUNK = 2 * ROWS + EXTRA
EPS = 1e-06
NEG = -1e30
SCALE = 1.0 / math.sqrt(HEAD_SIZE)
EXP2_SCALE = SCALE * math.log2(math.e)

SEQ = ("yl", "z", "core", "ep")
ROW = ("core", "ep")
REST = ("yl", "z", "tp")
F32 = jnp.float32
BF16 = jnp.bfloat16


def dot_nt(a, b):
    return lax.dot_general(a, b, (((1,), (1,)), ((), ())), preferred_element_type=F32)


def dot_nn(a, b):
    return lax.dot_general(a, b, (((1,), (0,)), ((), ())), preferred_element_type=F32)


def unit_of(raw):
    inverse = lax.rsqrt(jnp.mean(raw * raw, axis=-1, keepdims=True) + EPS)
    return raw * inverse, inverse


def norm_backward(grad, unit, inverse, gain):
    scaled = grad * gain
    inner = jnp.mean(scaled * unit, axis=-1, keepdims=True)
    return inverse * (scaled - unit * inner)


def fold(x):
    return jnp.sum(x.reshape(x.shape[0] // 8, 8, x.shape[1]), axis=0)


def split(x):
    high = x.astype(BF16)
    return high, (x - high.astype(F32)).astype(BF16)


def attention_kernel(
    here_ref, q_ref, g_ref, win_ref, seg_ref, qgain_ref, kgain_ref,
    qgrad_ref, parts_ref,
    kn, knt, bias, scores, dprob, probs_b, dscore, dk, dv, qsum,
):
    step = pl.program_id(0)
    qgain = qgain_ref[...]
    kgain = kgain_ref[...]

    @pl.when(step == 0)
    def _():
        here = here_ref[0]
        key_row = lax.broadcasted_iota(jnp.int32, (ROWS, ROWS), 0)
        query_col = lax.broadcasted_iota(jnp.int32, (ROWS, ROWS), 1)
        seg_q = jnp.broadcast_to(seg_ref[...].astype(F32), (ROWS, ROWS))
        for p in range(SPAN):
            rows = slice(p * ROWS, (p + 1) * ROWS)
            unit, _ = unit_of(win_ref[p, :ROWS, :].astype(F32))
            normed = (unit * kgain).astype(BF16)
            kn[rows, :] = normed
            knt[:, rows] = (unit * kgain).T.astype(BF16)
            marks = win_ref[p, 2 * ROWS : 2 * ROWS + EXTRA, :].astype(F32)[0:1, :]
            seg_k = jnp.broadcast_to(marks, (ROWS, ROWS)).T
            late = jnp.where(here == p, 1, 0) * key_row > query_col
            hidden = jnp.logical_or(seg_k != seg_q, late)
            bias[rows, :] = jnp.where(hidden, NEG, 0.0)
        dk[...] = jnp.zeros_like(dk)
        dv[...] = jnp.zeros_like(dv)
        qsum[...] = jnp.zeros_like(qsum)

    for pair in range(PAIRS):
        columns = [slice((2 * pair + h) * HEAD_SIZE, (2 * pair + h + 1) * HEAD_SIZE) for h in (0, 1)]
        units = [unit_of(q_ref[:, c].astype(F32)) for c in columns]
        normed = jnp.concatenate([(u * qgain).astype(BF16) for u, _ in units], axis=0)
        grads = jnp.concatenate([g_ref[:, c] for c in columns], axis=0)
        top8 = None
        for p in range(SPAN):
            rows = slice(p * ROWS, (p + 1) * ROWS)
            hide = bias[rows, :]
            s = dot_nt(kn[rows, :], normed) + jnp.concatenate([hide, hide], axis=1)
            scores[pair, rows, :] = s
            high = jnp.max(s.reshape(ROWS // 8, 8, 2 * ROWS), axis=0)
            top8 = high if top8 is None else jnp.maximum(top8, high)
        top = jnp.max(top8, axis=0, keepdims=True) * EXP2_SCALE
        total8 = jnp.zeros((8, 2 * ROWS), F32)
        for p in range(SPAN):
            rows = slice(p * ROWS, (p + 1) * ROWS)
            e = jnp.exp2(scores[pair, rows, :] * EXP2_SCALE - top)
            scores[pair, rows, :] = e
            total8 = total8 + fold(e)
            dprob[pair, rows, :] = dot_nt(win_ref[p, ROWS : 2 * ROWS, :], grads)
        inverse_total = 1.0 / jnp.sum(total8, axis=0, keepdims=True)
        delta8 = jnp.zeros((8, 2 * ROWS), F32)
        for p in range(SPAN):
            rows = slice(p * ROWS, (p + 1) * ROWS)
            rounded = (scores[pair, rows, :] * inverse_total).astype(BF16)
            probs_b[pair, rows, :] = rounded
            delta8 = delta8 + fold(rounded.astype(F32) * dprob[pair, rows, :])
        delta = jnp.sum(delta8, axis=0, keepdims=True)
        for p in range(SPAN):
            rows = slice(p * ROWS, (p + 1) * ROWS)
            prob = scores[pair, rows, :] * inverse_total
            dscore[pair, rows, :] = (prob * (dprob[pair, rows, :] - delta)).astype(BF16)
        dv[...] += dot_nn(probs_b[pair], grads)
        dk[...] += dot_nn(dscore[pair], normed)
        dq = dot_nn(knt[...], dscore[pair]).T * SCALE
        gain_rows = jnp.zeros((8, HEAD_SIZE), F32)
        for h in (0, 1):
            unit, inverse = units[h]
            part = dq[h * ROWS : (h + 1) * ROWS, :]
            qgrad_ref[:, columns[h]] = norm_backward(part, unit, inverse, qgain).astype(BF16)
            gain_rows = gain_rows + fold(part * unit)
        qsum[...] += gain_rows

    @pl.when(step == pl.num_programs(0) - 1)
    def _():
        ksum = jnp.zeros((8, HEAD_SIZE), F32)
        for p in range(SPAN):
            rows = slice(p * ROWS, (p + 1) * ROWS)
            unit, _ = unit_of(win_ref[p, :ROWS, :].astype(F32))
            part = dk[rows, :] * SCALE
            ksum = ksum + fold(part * unit)
            parts_ref[p, :ROWS, :] = part.astype(BF16)
            parts_ref[p, ROWS : 2 * ROWS, :] = dv[rows, :].astype(BF16)
        q_high, q_low = split(jnp.sum(qsum[...], axis=0, keepdims=True))
        k_high, k_low = split(jnp.sum(ksum, axis=0, keepdims=True))
        row = lax.broadcasted_iota(jnp.int32, (EXTRA, HEAD_SIZE), 0)
        extra = jnp.zeros((EXTRA, HEAD_SIZE), F32)
        for i, x in enumerate((q_high, q_low, k_high, k_low)):
            extra = jnp.where(row == i, x.astype(F32), extra)
        for p in range(SPAN):
            parts_ref[p, 2 * ROWS :, :] = extra.astype(BF16)


def attention(here, queries, gradient, window, segments, qgain, kgain):
    steps = HEADS // (2 * PAIRS)
    width = 2 * PAIRS * HEAD_SIZE
    whole = lambda shape: pl.BlockSpec(shape, lambda i: (0,) * len(shape))
    return pl.pallas_call(
        attention_kernel,
        grid=(steps,),
        in_specs=[
            pl.BlockSpec(memory_space=pltpu.SMEM),
            pl.BlockSpec((ROWS, width), lambda i: (0, i)),
            pl.BlockSpec((ROWS, width), lambda i: (0, i)),
            whole((SPAN, CHUNK, HEAD_SIZE)),
            whole((1, ROWS)),
            whole((1, HEAD_SIZE)),
            whole((1, HEAD_SIZE)),
        ],
        out_specs=[
            pl.BlockSpec((ROWS, width), lambda i: (0, i)),
            whole((SPAN, CHUNK, HEAD_SIZE)),
        ],
        out_shape=[
            jax.ShapeDtypeStruct((ROWS, HEADS * HEAD_SIZE), BF16),
            jax.ShapeDtypeStruct((SPAN, CHUNK, HEAD_SIZE), BF16),
        ],
        scratch_shapes=[
            pltpu.VMEM((TOKENS, HEAD_SIZE), BF16),
            pltpu.VMEM((HEAD_SIZE, TOKENS), BF16),
            pltpu.VMEM((TOKENS, ROWS), F32),
            pltpu.VMEM((PAIRS, TOKENS, 2 * ROWS), F32),
            pltpu.VMEM((PAIRS, TOKENS, 2 * ROWS), F32),
            pltpu.VMEM((PAIRS, TOKENS, 2 * ROWS), BF16),
            pltpu.VMEM((PAIRS, TOKENS, 2 * ROWS), BF16),
            pltpu.VMEM((TOKENS, HEAD_SIZE), F32),
            pltpu.VMEM((TOKENS, HEAD_SIZE), F32),
            pltpu.VMEM((8, HEAD_SIZE), F32),
        ],
        compiler_params=pltpu.CompilerParams(vmem_limit_bytes=40 * 2**20),
        name="attention_backward",
    )(here, queries, gradient, window, segments, qgain, kgain)


def combine_kernel(here_ref, parts_ref, own_ref, prev_ref, sums_ref):
    here = here_ref[0]
    for block in (0, 1):
        rows = slice(block * ROWS, (block + 1) * ROWS)
        own = jnp.zeros((ROWS, HEAD_SIZE), F32)
        prev = jnp.zeros((ROWS, HEAD_SIZE), F32)
        for p in range(SPAN):
            part = parts_ref[p, rows, :].astype(F32)
            is_own = p >= here
            own = own + jnp.where(is_own, part, 0.0)
            prev = prev + jnp.where(is_own, 0.0, part)
        own_ref[rows, :] = own
        prev_ref[rows, :] = prev.astype(BF16)
    extra = jnp.zeros((EXTRA, HEAD_SIZE), F32)
    for p in range(SPAN):
        extra = extra + parts_ref[p, 2 * ROWS :, :].astype(F32)
    qsum = extra[0:1, :] + extra[1:2, :]
    ksum = extra[2:3, :] + extra[3:4, :]
    both = jnp.concatenate([qsum, ksum], axis=0)
    sums_ref[...] = jnp.broadcast_to(both[None], sums_ref.shape)


def final_kernel(factor, own_ref, back_ref, key_ref, kgain_ref, sums_ref, kgrad_ref, vgrad_ref, gq_ref, gk_ref):
    unit, inverse = unit_of(key_ref[...].astype(F32))
    dk = own_ref[:ROWS, :] + back_ref[:ROWS, :].astype(F32)
    kgrad_ref[...] = norm_backward(dk, unit, inverse, kgain_ref[...]).astype(BF16)
    vgrad_ref[...] = (own_ref[ROWS:, :] + back_ref[ROWS:, :].astype(F32)).astype(BF16)
    sums = jnp.sum(sums_ref[...], axis=0) * factor
    gq_ref[...] = sums[0:1, :]
    gk_ref[...] = sums[1:2, :]


def per_device(queries, keys, value, gradient, segments, qgain, kgain):
    here = lax.axis_index(ROW)
    rest = lax.axis_size(REST)
    seq = lax.axis_size(SEQ)
    qgain, kgain = qgain.reshape(1, -1), kgain.reshape(1, -1)
    marks = jnp.broadcast_to(segments.astype(BF16)[None], (EXTRA, ROWS))
    own = jnp.concatenate([keys, value, marks], axis=0)
    previous = lax.ppermute(own, SEQ, [(i, (i + SPAN) % seq) for i in range(seq)])
    is_own = jnp.arange(SPAN) >= here
    outgoing = jnp.where(is_own[:, None, None], own[None], previous[None])
    window = lax.all_to_all(outgoing, ROW, 0, 0)
    place = here.astype(jnp.int32).reshape(1)
    qgrad, parts = attention(place, queries, gradient, window, segments.reshape(1, -1), qgain, kgain)
    returned = lax.all_to_all(parts, ROW, 0, 0)
    smem = pl.BlockSpec(memory_space=pltpu.SMEM)
    vmem = pl.BlockSpec(memory_space=pltpu.VMEM)
    mine, prev, sums = pl.pallas_call(
        combine_kernel,
        in_specs=[smem, vmem],
        out_specs=[vmem] * 3,
        out_shape=[
            jax.ShapeDtypeStruct((2 * ROWS, HEAD_SIZE), F32),
            jax.ShapeDtypeStruct((2 * ROWS, HEAD_SIZE), BF16),
            jax.ShapeDtypeStruct((rest, 2, HEAD_SIZE), F32),
        ],
        name="combine_partials",
    )(place, returned)
    back = lax.ppermute(prev, SEQ, [((i + SPAN) % seq, i) for i in range(seq)])
    sums = lax.all_to_all(sums, REST, 0, 0)
    factor = 1.0 / math.sqrt(ROWS * seq * HEADS * lax.axis_size("tp"))
    kgrad, vgrad, gq, gk = pl.pallas_call(
        lambda *refs: final_kernel(factor, *refs),
        in_specs=[vmem] * 5,
        out_specs=[vmem] * 4,
        out_shape=[
            jax.ShapeDtypeStruct((ROWS, HEAD_SIZE), BF16),
            jax.ShapeDtypeStruct((ROWS, HEAD_SIZE), BF16),
            jax.ShapeDtypeStruct((1, HEAD_SIZE), F32),
            jax.ShapeDtypeStruct((1, HEAD_SIZE), F32),
        ],
        name="finish_gradients",
    )(mine, back, keys, kgain, sums)
    return qgrad, kgrad, vgrad, gq.reshape(-1), gk.reshape(-1)


def solution(mesh):
    outer, ep, tp = mesh.devices.shape
    fine = Mesh(
        mesh.devices.reshape(2, outer // 4, 2, ep, tp), ("yl", "z", "core", "ep", "tp")
    )
    tokens = P(SEQ, "tp")
    return jax.shard_map(
        per_device,
        mesh=fine,
        in_specs=(tokens, tokens, tokens, tokens, P(SEQ), P(), P()),
        out_specs=(tokens, tokens, tokens, P(), P()),
        check_vma=False,
    )
```

time: 279 us -> 90.7 us (0.33)
  starting transfers between devices: 128 us -> 20.4 us
  blocking collectives: 107 us -> 28.4 us
  matrix products: 20.8 us -> 0 us
  waiting for transfers between devices: 5.01 us -> 22 us
  Pallas kernels: 0 us -> 15.7 us
  local copies, waits for them, and re-layouts: 7.74 us -> 1.32 us
  other arithmetic: 7.15 us -> 1.56 us
    ppermute x35 -> x2, starting transfers between devices: 128 us -> 8.82 us  [the longest x1 4.55 us: per_device(): back = lax.ppermute(prev, SEQ, [((i + SPAN) % seq, i) for i in range(seq)])]
    psum x1 -> x0, blocking collectives: 107 us -> none  [per_device(): lax.psum((local_query, local_key), ('outer', 'ep', 'tp'))]
    all_to_all x0 -> x2, blocking collectives: none -> 28.4 us  [the longest x1 14.8 us: per_device(): window = lax.all_to_all(outgoing, ROW, 0, 0)]
    dot_general x48 -> x0, matrix products: 20.8 us -> none  [the longest x8 6.36 us: per_device(): jnp.einsum('hgqk,qhgd->khd', block_probs_b, gradient_list, preferred_elem...]
    pallas_call x0 -> x3, Pallas kernels: none -> 15.7 us  [the longest x1 11.9 us: attention(): pl.pallas_call(attention_kernel, grid=(steps,), in_specs=[pl.BlockSpec(me...]
    all_to_all x0 -> x1, starting transfers between devices: none -> 11.6 us  [per_device(): sums = lax.all_to_all(sums, REST, 0, 0)]
    ppermute x35 -> x2, waiting for transfers between devices: 5.01 us -> 14.4 us  [the longest x1 12.4 us: per_device(): lax.ppermute(own, SEQ, [(i, (i + SPAN) % seq) for i in range(seq)])]
    all_to_all x0 -> x1, waiting for transfers between devices: none -> 7.68 us  [per_device(): sums = lax.all_to_all(sums, REST, 0, 0)]
  transfers between devices with their start and end apart: 35 -> 3, of which waited for: 3 -> 3; matrix products, arithmetic and copies ran while one was open for 11% -> 0% of each run, Pallas kernels for 0% -> 0%
where the time goes in v1:
time: 90.7 us; the launch traced here: 90.2 us
  blocking collectives  28.4 us (31%)
  waiting for transfers between devices  22 us (24%)
  starting transfers between devices  20.4 us (22%)
  Pallas kernels  15.7 us (17%)
  other arithmetic  1.56 us (2%)
  local copies, waits for them, and re-layouts  1.32 us (1%)
    all_to_all x1, blocking collectives, per_device(): window = lax.all_to_all(outgoing, ROW, 0, 0)  14.8 us
    all_to_all x1, blocking collectives, per_device(): returned = lax.all_to_all(parts, ROW, 0, 0)  13.6 us
    ppermute x1, waiting for transfers between devices, per_device(): lax.ppermute(own, SEQ, [(i, (i + SPAN) % seq) for i in range(seq)])  12.4 us
    pallas_call x1, Pallas kernels, attention(): pl.pallas_call(attention_kernel, grid=(steps,), in_specs=[pl.BlockSpec(me...  11.9 us
    all_to_all x1, starting transfers between devices, per_device(): sums = lax.all_to_all(sums, REST, 0, 0)  11.6 us
    all_to_all x1, waiting for transfers between devices, per_device(): sums = lax.all_to_all(sums, REST, 0, 0)  7.68 us
    ppermute x1, starting transfers between devices, per_device(): back = lax.ppermute(prev, SEQ, [((i + SPAN) % seq, i) for i in range(seq)])  4.55 us
    ppermute x1, starting transfers between devices, per_device(): lax.ppermute(own, SEQ, [(i, (i + SPAN) % seq) for i in range(seq)])  4.27 us
  transfers between devices with their start and end apart: 3, of which 3 were waited for; matrix products, arithmetic and copies ran while one was open for 0% of the time, Pallas kernels for 0%

profile of v1, /device:TPU:8, one launch (start us, length us, event | category | flops | bytes accessed | tf_op | source)
XLA Modules:
  0.0 90.2 jit_solution(6066622849119068813)
XLA Ops:
  0.6 0.7 convert_element_type.3
  1.3 0.8 pad_maximum_fusion
  2.1 4.3 %collective-permute-start = (bf16[272,128]{1,0:T(8,128)(2,1)S(1)}, bf16[272,128]{1,0:T(8,128)(2,1)S(1)}, u32[]{:S(2)}, u32[]{:S(2)}) collective-permute-start(bf16[272,128]{1,0:T(8,128)(2,1)S(1)} %pad_maximum_fusion), channel_id=1, source_target_pairs={{0,32},{4,36},{8,40},{12,44},{16,48},{20,52},{24,56},{28,60},{32,6... | collective-permute-start | bytes 208904 | tf_op jit(solution)/shard_map/ppermute | solution.py:233
  6.4 12.4 %collective-permute-done = bf16[272,128]{1,0:T(8,128)(2,1)S(1)} collective-permute-done((bf16[272,128]{1,0:T(8,128)(2,1)S(1)}, bf16[272,128]{1,0:T(8,128)(2,1)S(1)}, u32[]{:S(2)}, u32[]{:S(2)}) %collective-permute-start) | collective-permute-done | bytes 69664 | tf_op jit(solution)/shard_map/ppermute | solution.py:233
  18.8 0.1 broadcast_select_fusion
  18.9 0.0 copy-start
  18.9 0.0 copy-start.1
  19.0 14.8 %all_to_all.15.win_ref = bf16[8,272,128]{2,1,0:T(8,128)(2,1)S(1)} all-to-all(bf16[8,272,128]{2,1,0:T(8,128)(2,1)S(1)} %broadcast_select_fusion), channel_id=1, replica_groups=mesh['yl'=2,'z'=12,'core'=2,'ep'=4,'tp'=4] {'core','ep'}, dimensions={0} | all-to-all | bytes 1114112 | tf_op jit(solution)/shard_map/all_to_all | solution.py:236
  33.8 0.0 copy-start.2
  33.8 0.0 copy-start.3
  33.8 0.0 copy-start.4
  33.8 0.0 copy-done
  33.8 0.0 copy-done.1
  33.8 0.6 copy-done.2
  34.4 0.0 copy-done.3
  34.4 0.0 copy-done.4
  34.5 11.9 %attention_backward.1 = (bf16[128,2048]{1,0:T(8,128)(2,1)}, bf16[8,272,128]{2,1,0:T(8,128)(2,1)S(1)}) custom-call(s32[1]{0:T(128)} %bitcast.here_ref, bf16[128,2048]{1,0:T(8,128)(2,1)S(1)} %copy-done, bf16[128,2048]{1,0:T(8,128)(2,1)S(1)} %copy-done.1, bf16[8,272,128]{2,1,0:T(8,128)(2,1)S(1)} %all_to_all.15.win_ref, s32[1,128]{1,0:T(1,128)S(1)} %bitcast.8, ...), custom_call_target="tpu_custom_call" | custom-call | tf_op jit(solution)/shard_map/attention_backward/pallas_call | solution.py:157
  46.4 13.6 %all_to_all.16.parts_ref = bf16[8,272,128]{2,1,0:T(8,128)(2,1)} all-to-all(bf16[8,272,128]{2,1,0:T(8,128)(2,1)S(1)} %get-tuple-element.15), channel_id=1, replica_groups=mesh['yl'=2,'z'=12,'core'=2,'ep'=4,'tp'=4] {'core','ep'}, dimensions={0} | all-to-all | bytes 1114112 | tf_op jit(solution)/shard_map/all_to_all | solution.py:239
  60.0 2.0 %combine_partials.1 = (f32[256,128]{1,0:T(8,128)}, bf16[256,128]{1,0:T(8,128)(2,1)}, f32[96,2,128]{2,1,0:T(2,128)}) custom-call(s32[1]{0:T(128)} %bitcast.here_ref, bf16[8,272,128]{2,1,0:T(8,128)(2,1)} %all_to_all.16.parts_ref), custom_call_target="tpu_custom_call" | custom-call | tf_op jit(solution)/shard_map/combine_partials/pallas_call | solution.py:242
  62.0 0.0 copy-start.7
  62.0 11.6 %all-to-all-start.2 = ((f32[96,2,128]{2,1,0:T(2,128)}), f32[96,2,128]{2,1,0:T(2,128)S(1)}, u32[]{:S(2)}, u32[]{:S(2)}) async-start(f32[96,2,128]{2,1,0:T(2,128)} %get-tuple-element.18), calls=%async_computation.2 | async-start | bytes 196608 | tf_op jit(solution)/shard_map/all_to_all | solution.py:254
  73.6 0.0 copy-done.7
  73.6 4.6 %collective-permute-start.1 = (bf16[256,128]{1,0:T(8,128)(2,1)S(1)}, bf16[256,128]{1,0:T(8,128)(2,1)S(1)}, u32[]{:S(2)}, u32[]{:S(2)}) collective-permute-start(bf16[256,128]{1,0:T(8,128)(2,1)S(1)} %copy-done.7), channel_id=1, source_target_pairs={{32,0},{36,4},{40,8},{44,12},{48,16},{52,20},{56,24},{60,28},{64,3... | collective-permute-start | bytes 196616 | tf_op jit(solution)/shard_map/ppermute | solution.py:253
  78.2 1.9 %collective-permute-done.1.refs_1_ = bf16[256,128]{1,0:T(8,128)(2,1)S(1)} collective-permute-done((bf16[256,128]{1,0:T(8,128)(2,1)S(1)}, bf16[256,128]{1,0:T(8,128)(2,1)S(1)}, u32[]{:S(2)}, u32[]{:S(2)}) %collective-permute-start.1) | collective-permute-done | bytes 65568 | tf_op jit(solution)/shard_map/ppermute | solution.py:253
  80.1 0.0 copy-start.6
  80.1 7.7 %all-to-all-done.2.refs_4_ = f32[96,2,128]{2,1,0:T(2,128)S(1)} async-done(((f32[96,2,128]{2,1,0:T(2,128)}), f32[96,2,128]{2,1,0:T(2,128)S(1)}, u32[]{:S(2)}, u32[]{:S(2)}) %all-to-all-start.2) | async-done | bytes 98336 | tf_op jit(solution)/shard_map/all_to_all | solution.py:254
  87.8 0.0 copy-start.5
  87.8 0.0 copy-done.6
  87.8 0.6 copy-done.5
  88.4 1.8 %finish_gradients.1 = (bf16[128,128]{1,0:T(8,128)(2,1)}, bf16[128,128]{1,0:T(8,128)(2,1)}, f32[1,128]{1,0:T(1,128)}, f32[1,128]{1,0:T(1,128)}) custom-call(f32[256,128]{1,0:T(8,128)} %get-tuple-element.16.refs_0_, bf16[256,128]{1,0:T(8,128)(2,1)} %copy-done.6, bf16[128,128]{1,0:T(8,128)(2,1)} %refs_2_.1, f32[1,128]{1,0:T(1,128)} %bitcast.6, ...), custom_call_target="tpu_custom_call" | custom-call | tf_op jit(solution)/shard_map/finish_gradients/pallas_call | solution.py:256
  (2 shorter events, 0.0 us)
Async XLA Ops:
  2.1 16.7 %collective-permute-start = (bf16[272,128]{1,0:T(8,128)(2,1)S(1)}, bf16[272,128]{1,0:T(8,128)(2,1)S(1)}, u32[]{:S(2)}, u32[]{:S(2)}) collective-permute-start(bf16[272,128]{1,0:T(8,128)(2,1)S(1)} %pad_maximum_fusion), channel_id=1, source_target_pairs={{0,32},{4,36},{8,40},{12,44},{16,48},{20,52},{24,56},{28,60},{32,6... | collective-permute-start | bytes 208904 | tf_op jit(solution)/shard_map/ppermute | solution.py:233
  18.9 14.8 %copy-start = (bf16[128,2048]{1,0:T(8,128)(2,1)S(1)}, bf16[128,2048]{1,0:T(8,128)(2,1)}, u32[]{:S(2)}) copy-start(bf16[128,2048]{1,0:T(8,128)(2,1)} %q_ref.1) | copy-start | bytes 1572868
  18.9 14.8 %copy-start.1 = (bf16[128,2048]{1,0:T(8,128)(2,1)S(1)}, bf16[128,2048]{1,0:T(8,128)(2,1)}, u32[]{:S(2)}) copy-start(bf16[128,2048]{1,0:T(8,128)(2,1)} %g_ref.1) | copy-start | bytes 1572868
  33.8 0.7 copy-start.2
  33.8 0.7 copy-start.3
  33.8 0.7 copy-start.4
  62.0 11.6 %copy-start.7 = (bf16[256,128]{1,0:T(8,128)(2,1)S(1)}, bf16[256,128]{1,0:T(8,128)(2,1)}, u32[]{:S(2)}) copy-start(bf16[256,128]{1,0:T(8,128)(2,1)} %get-tuple-element.17) | copy-start | bytes 196612
  62.0 25.7 %all-to-all-start.2 = ((f32[96,2,128]{2,1,0:T(2,128)}), f32[96,2,128]{2,1,0:T(2,128)S(1)}, u32[]{:S(2)}, u32[]{:S(2)}) async-start(f32[96,2,128]{2,1,0:T(2,128)} %get-tuple-element.18), calls=%async_computation.2 | async-start | bytes 196608 | tf_op jit(solution)/shard_map/all_to_all | solution.py:254
  73.6 6.5 %collective-permute-start.1 = (bf16[256,128]{1,0:T(8,128)(2,1)S(1)}, bf16[256,128]{1,0:T(8,128)(2,1)S(1)}, u32[]{:S(2)}, u32[]{:S(2)}) collective-permute-start(bf16[256,128]{1,0:T(8,128)(2,1)S(1)} %copy-done.7), channel_id=1, source_target_pairs={{32,0},{36,4},{40,8},{44,12},{48,16},{52,20},{56,24},{60,28},{64,3... | collective-permute-start | bytes 196616 | tf_op jit(solution)/shard_map/ppermute | solution.py:253
  80.1 7.7 %copy-start.6 = (bf16[256,128]{1,0:T(8,128)(2,1)}, bf16[256,128]{1,0:T(8,128)(2,1)S(1)}, u32[]{:S(2)}) copy-start(bf16[256,128]{1,0:T(8,128)(2,1)S(1)} %collective-permute-done.1.refs_1_) | copy-start | bytes 196612
  87.8 0.6 copy-start.5

commit v2 on v1

v2 whole, which is shorter than its diff:
```python
import math

import jax
import jax.numpy as jnp
from jax import lax
from jax.experimental import pallas as pl
from jax.experimental.pallas import tpu as pltpu
from jax.sharding import Mesh
from jax.sharding import PartitionSpec as P

HEAD_SIZE = 128
ROWS = 128
SPAN = 8
HEADS = 16
WIDE = 256
GROUPS = HEADS * ROWS // WIDE
TOKENS = SPAN * ROWS
EXTRA = 16
CHUNK = 2 * ROWS + EXTRA
EPS = 1e-06
NEG = -1e30
SCALE = 1.0 / math.sqrt(HEAD_SIZE)
EXP2_SCALE = SCALE * math.log2(math.e)

SEQ = ("yl", "z", "core", "ep")
ROW = ("core", "ep")
REST = ("yl", "z", "tp")
F32 = jnp.float32
BF16 = jnp.bfloat16


def dot_nt(a, b):
    return lax.dot_general(a, b, (((1,), (1,)), ((), ())), preferred_element_type=F32)


def dot_nn(a, b):
    return lax.dot_general(a, b, (((1,), (0,)), ((), ())), preferred_element_type=F32)


def unit_of(raw):
    inverse = lax.rsqrt(jnp.mean(raw * raw, axis=-1, keepdims=True) + EPS)
    return raw * inverse, inverse


def norm_backward(grad, unit, inverse, gain):
    scaled = grad * gain
    inner = jnp.mean(scaled * unit, axis=-1, keepdims=True)
    return inverse * (scaled - unit * inner)


def fold(x):
    return jnp.sum(x.reshape(x.shape[0] // 8, 8, x.shape[1]), axis=0)


def split(x):
    high = x.astype(BF16)
    return high, (x - high.astype(F32)).astype(BF16)


def interleave(*work):
    work = list(work)
    while work:
        for steps in list(work):
            if next(steps, steps) is steps:
                work.remove(steps)


def prepare_kernel(q_ref, g_ref, qgain_ref, kgain_ref, qn_ref, gh_ref, gains_ref):
    qgain = qgain_ref[...]
    for h in range(HEADS):
        columns = slice(h * HEAD_SIZE, (h + 1) * HEAD_SIZE)
        rows = slice(h * ROWS, (h + 1) * ROWS)
        unit, _ = unit_of(q_ref[:, columns].astype(F32))
        qn_ref[rows, :] = (unit * qgain).astype(BF16)
        gh_ref[rows, :] = g_ref[:, columns]
    row = lax.broadcasted_iota(jnp.int32, (8, HEAD_SIZE), 0)
    gains_ref[...] = jnp.where(row == 0, qgain, kgain_ref[...])


def attention_kernel(
    here_ref, qn_ref, g_ref, win_ref, own_ref, gains_ref,
    parts_ref, dqt_ref,
    kn, knt, vals, bias, scores, dprob, probs_b, dscore, dk, dv,
):
    qgain = gains_ref[0:1, :]
    kgain = gains_ref[1:2, :]
    here = here_ref[0]
    key_row = lax.broadcasted_iota(jnp.int32, (ROWS, ROWS), 0)
    query_col = lax.broadcasted_iota(jnp.int32, (ROWS, ROWS), 1)
    seg_q = jnp.broadcast_to(own_ref[2 * ROWS :, :].astype(F32)[0:1, :], (ROWS, ROWS))
    for p in range(SPAN):
        rows = slice(p * ROWS, (p + 1) * ROWS)
        unit, _ = unit_of(win_ref[p, :ROWS, :].astype(F32))
        normed = unit * kgain
        kn[rows, :] = normed.astype(BF16)
        knt[:, rows] = normed.T.astype(BF16)
        vals[rows, :] = win_ref[p, ROWS : 2 * ROWS, :]
        marks = win_ref[p, 2 * ROWS : 2 * ROWS + EXTRA, :].astype(F32)[0:1, :]
        seg_k = jnp.broadcast_to(marks, (ROWS, ROWS)).T
        late = jnp.where(here == p, 1, 0) * key_row > query_col
        hidden = jnp.logical_or(seg_k != seg_q, late)
        bias[rows, :] = jnp.where(hidden, NEG, 0.0)

    blocks = [slice(p * ROWS, (p + 1) * ROWS) for p in range(SPAN)]
    totals = [None] * GROUPS

    def softmax_steps(n):
        slot, cols = n % 2, slice(n * WIDE, (n + 1) * WIDE)
        top8 = jnp.full((8, WIDE), 2 * NEG, F32)
        for rows in blocks:
            hide = jnp.concatenate([bias[rows, :]] * (WIDE // ROWS), axis=1)
            s = dot_nt(kn[rows, :], qn_ref[cols, :]) + hide
            scores[slot, rows, :] = s
            top8 = jnp.maximum(top8, jnp.max(s.reshape(ROWS // 8, 8, WIDE), axis=0))
            yield
        top = jnp.max(top8, axis=0, keepdims=True) * EXP2_SCALE
        total8 = jnp.zeros((8, WIDE), F32)
        for rows in blocks:
            e = jnp.exp2(scores[slot, rows, :] * EXP2_SCALE - top)
            scores[slot, rows, :] = e
            total8 = total8 + fold(e)
            yield
        totals[n] = jnp.sum(total8, axis=0, keepdims=True)

    def gradient_steps(n):
        slot, cols = n % 2, slice(n * WIDE, (n + 1) * WIDE)
        inverse_total = 1.0 / totals[n]
        delta8 = jnp.zeros((8, WIDE), F32)
        for rows in blocks:
            rounded = (scores[slot, rows, :] * inverse_total).astype(BF16)
            probs_b[slot, rows, :] = rounded
            d = dot_nt(vals[rows, :], g_ref[cols, :])
            dprob[rows, :] = d
            delta8 = delta8 + fold(rounded.astype(F32) * d)
            yield
        delta = jnp.sum(delta8, axis=0, keepdims=True)
        for rows in blocks:
            prob = scores[slot, rows, :] * inverse_total
            dscore[slot, rows, :] = (prob * (dprob[rows, :] - delta)).astype(BF16)
            yield

    def sum_steps(n):
        slot, cols = n % 2, slice(n * WIDE, (n + 1) * WIDE)
        for rows in (slice(0, TOKENS // 2), slice(TOKENS // 2, TOKENS)):
            v = dot_nn(probs_b[slot, rows, :], g_ref[cols, :])
            dv[rows, :] = v if n == 0 else dv[rows, :] + v
            yield
        for rows in (slice(0, TOKENS // 2), slice(TOKENS // 2, TOKENS)):
            k = dot_nn(dscore[slot, rows, :], qn_ref[cols, :])
            dk[rows, :] = k if n == 0 else dk[rows, :] + k
            yield
        dqt_ref[:, cols] = dot_nn(knt[...], dscore[slot]) * SCALE
        yield

    interleave(softmax_steps(0))
    for n in range(GROUPS):
        work = [gradient_steps(n)]
        if n + 1 < GROUPS:
            work.append(softmax_steps(n + 1))
        if n:
            work.append(sum_steps(n - 1))
        interleave(*work)
    interleave(sum_steps(GROUPS - 1))

    ksum = jnp.zeros((8, HEAD_SIZE), F32)
    qsum = jnp.zeros((8, HEAD_SIZE), F32)
    for p, rows in enumerate(blocks):
        unit, _ = unit_of(win_ref[p, :ROWS, :].astype(F32))
        part = dk[rows, :] * SCALE
        ksum = ksum + fold(part * unit)
        qsum = qsum + fold(part * kn[rows, :].astype(F32))
        parts_ref[p, :ROWS, :] = part.astype(BF16)
        parts_ref[p, ROWS : 2 * ROWS, :] = dv[rows, :].astype(BF16)
    q_high, q_low = split(jnp.sum(qsum, axis=0, keepdims=True) / qgain)
    k_high, k_low = split(jnp.sum(ksum, axis=0, keepdims=True))
    row = lax.broadcasted_iota(jnp.int32, (EXTRA, HEAD_SIZE), 0)
    extra = jnp.zeros((EXTRA, HEAD_SIZE), F32)
    for i, x in enumerate((q_high, q_low, k_high, k_low)):
        extra = jnp.where(row == i, x.astype(F32), extra)
    for p in range(SPAN):
        parts_ref[p, 2 * ROWS :, :] = extra.astype(BF16)


def finish_query_kernel(dqt_ref, q_ref, qgain_ref, qgrad_ref):
    qgain = qgain_ref[...]
    for h in range(HEADS):
        columns = slice(h * HEAD_SIZE, (h + 1) * HEAD_SIZE)
        unit, inverse = unit_of(q_ref[:, columns].astype(F32))
        dq = dqt_ref[:, h * ROWS : (h + 1) * ROWS].T
        qgrad_ref[:, columns] = norm_backward(dq, unit, inverse, qgain).astype(BF16)


def combine_kernel(here_ref, parts_ref, own_ref, prev_ref, sums_ref):
    here = here_ref[0]
    for block in (0, 1):
        rows = slice(block * ROWS, (block + 1) * ROWS)
        own = jnp.zeros((ROWS, HEAD_SIZE), F32)
        prev = jnp.zeros((ROWS, HEAD_SIZE), F32)
        for p in range(SPAN):
            part = parts_ref[p, rows, :].astype(F32)
            is_own = p >= here
            own = own + jnp.where(is_own, part, 0.0)
            prev = prev + jnp.where(is_own, 0.0, part)
        own_ref[rows, :] = own
        prev_ref[rows, :] = prev.astype(BF16)
    extra = jnp.zeros((EXTRA, HEAD_SIZE), F32)
    for p in range(SPAN):
        extra = extra + parts_ref[p, 2 * ROWS :, :].astype(F32)
    qsum = extra[0:1, :] + extra[1:2, :]
    ksum = extra[2:3, :] + extra[3:4, :]
    both = jnp.concatenate([qsum, ksum], axis=0)
    sums_ref[...] = jnp.broadcast_to(both[None], sums_ref.shape)


def finish_key_kernel(own_ref, back_ref, key_ref, kgain_ref, kgrad_ref, vgrad_ref):
    unit, inverse = unit_of(key_ref[...].astype(F32))
    dk = own_ref[:ROWS, :] + back_ref[:ROWS, :].astype(F32)
    kgrad_ref[...] = norm_backward(dk, unit, inverse, kgain_ref[...]).astype(BF16)
    vgrad_ref[...] = (own_ref[ROWS:, :] + back_ref[ROWS:, :].astype(F32)).astype(BF16)


VMEM = pl.BlockSpec(memory_space=pltpu.VMEM)
SMEM = pl.BlockSpec(memory_space=pltpu.SMEM)


def call(kernel, name, operands, outs, mib, scratch=(), flops=0, data=0, scalar=False):
    return pl.pallas_call(
        kernel,
        in_specs=([SMEM] if scalar else []) + [VMEM] * (len(operands) - scalar),
        out_specs=[VMEM] * len(outs),
        out_shape=[jax.ShapeDtypeStruct(*out) for out in outs],
        scratch_shapes=list(scratch),
        compiler_params=pltpu.CompilerParams(vmem_limit_bytes=mib * 2**20),
        cost_estimate=pl.CostEstimate(flops=flops, bytes_accessed=data, transcendentals=0),
        name=name,
    )(*operands)


def per_device(queries, keys, value, gradient, segments, qgain, kgain):
    here = lax.axis_index(ROW)
    rest = lax.axis_size(REST)
    seq = lax.axis_size(SEQ)
    heads = HEADS * ROWS
    qgain, kgain = qgain.reshape(1, -1), kgain.reshape(1, -1)
    marks = jnp.broadcast_to(segments.astype(BF16)[None], (EXTRA, ROWS))
    own = jnp.concatenate([keys, value, marks], axis=0)
    previous = lax.ppermute(own, SEQ, [(i, (i + SPAN) % seq) for i in range(seq)])
    normed, gradient, gains = call(
        prepare_kernel, "prepare_queries", (queries, gradient, qgain, kgain),
        [((heads, HEAD_SIZE), BF16), ((heads, HEAD_SIZE), BF16), ((8, HEAD_SIZE), F32)],
        4, flops=10**9, data=2 * 10**6,
    )
    previous, normed, gradient, gains = lax.optimization_barrier((previous, normed, gradient, gains))
    is_own = jnp.arange(SPAN) >= here
    outgoing = jnp.where(is_own[:, None, None], own[None], previous[None])
    window = lax.all_to_all(outgoing, ROW, 0, 0)
    place = here.astype(jnp.int32).reshape(1)
    parts, dqt = call(
        attention_kernel, "attention_backward", (place, normed, gradient, window, own, gains),
        [((SPAN, CHUNK, HEAD_SIZE), BF16), ((HEAD_SIZE, heads), F32)],
        16,
        scratch=[
            pltpu.VMEM((TOKENS, HEAD_SIZE), BF16),
            pltpu.VMEM((HEAD_SIZE, TOKENS), BF16),
            pltpu.VMEM((TOKENS, HEAD_SIZE), BF16),
            pltpu.VMEM((TOKENS, ROWS), F32),
            pltpu.VMEM((2, TOKENS, WIDE), F32),
            pltpu.VMEM((TOKENS, WIDE), F32),
            pltpu.VMEM((2, TOKENS, WIDE), BF16),
            pltpu.VMEM((2, TOKENS, WIDE), BF16),
            pltpu.VMEM((TOKENS, HEAD_SIZE), F32),
            pltpu.VMEM((TOKENS, HEAD_SIZE), F32),
        ],
        flops=4 * 10**9, data=10**7, scalar=True,
    )
    returned = lax.all_to_all(parts, ROW, 0, 0)
    (qgrad,) = call(
        finish_query_kernel, "finish_queries", (dqt, queries, qgain),
        [((ROWS, heads), BF16)], 4, flops=10**9, data=2 * 10**6,
    )
    mine, prev, sums = call(
        combine_kernel, "combine_partials", (place, returned),
        [((2 * ROWS, HEAD_SIZE), F32), ((2 * ROWS, HEAD_SIZE), BF16), ((rest, 2, HEAD_SIZE), F32)],
        4, flops=10**8, data=10**6, scalar=True,
    )
    back = lax.ppermute(prev, SEQ, [((i + SPAN) % seq, i) for i in range(seq)])
    sums = lax.all_to_all(sums, REST, 0, 0)
    kgrad, vgrad = call(
        finish_key_kernel, "finish_keys", (mine, back, keys, kgain),
        [((ROWS, HEAD_SIZE), BF16), ((ROWS, HEAD_SIZE), BF16)], 4, flops=10**8, data=10**6,
    )
    factor = 1.0 / math.sqrt(ROWS * seq * HEADS * lax.axis_size("tp"))
    sums = jnp.sum(sums, axis=0) * factor
    return qgrad, kgrad, vgrad, sums[0], sums[1]


def solution(mesh):
    outer, ep, tp = mesh.devices.shape
    fine = Mesh(
        mesh.devices.reshape(2, outer // 4, 2, ep, tp), ("yl", "z", "core", "ep", "tp")
    )
    tokens = P(SEQ, "tp")
    return jax.shard_map(
        per_device,
        mesh=fine,
        in_specs=(tokens, tokens, tokens, tokens, P(SEQ), P(), P()),
        out_specs=(tokens, tokens, tokens, P(), P()),
        check_vma=False,
    )
```

time: 90.7 us -> 81.7 us (0.901)
  waiting for transfers between devices: 22 us -> 15 us
  Pallas kernels: 15.7 us -> 12.3 us
  local copies, waits for them, and re-layouts: 1.32 us -> 3.28 us
    pallas_call x3 -> x5, Pallas kernels: 15.7 us -> 12.3 us  [call(): pl.pallas_call(kernel, in_specs=([SMEM] if scalar else []) + [VMEM] * (le...]
    ppermute x1, waiting for transfers between devices: 12.4 us -> 9.28 us  [per_device(): lax.ppermute(own, SEQ, [(i, (i + SPAN) % seq) for i in range(seq)])]
    all_to_all x1, waiting for transfers between devices: 7.68 us -> 5.7 us  [per_device(): sums = lax.all_to_all(sums, REST, 0, 0)]
    ppermute x1, waiting for transfers between devices: 1.92 us -> 0.01 us  [per_device(): back = lax.ppermute(prev, SEQ, [((i + SPAN) % seq, i) for i in range(seq)])]
    unnamed x16 -> x12, local copies, waits for them, and re-layouts: 1.32 us -> 2.75 us
  transfers between devices with their start and end apart: 3 -> 3, of which waited for: 3 -> 2; matrix products, arithmetic and copies ran while one was open for 0% -> 0% of each run, Pallas kernels for 0% -> 5%
where the time goes in v2:
time: 81.7 us; the launch traced here: 81.2 us
  blocking collectives  27.6 us (34%)
  starting transfers between devices  20.6 us (25%)
  waiting for transfers between devices  15 us (18%)
  Pallas kernels  12.3 us (15%)
  local copies, waits for them, and re-layouts  3.28 us (4%)
  other arithmetic  1.67 us (2%)
    all_to_all x1, blocking collectives, per_device(): window = lax.all_to_all(outgoing, ROW, 0, 0)  14.7 us
    all_to_all x1, blocking collectives, per_device(): returned = lax.all_to_all(parts, ROW, 0, 0)  12.9 us
    pallas_call x5, Pallas kernels, call(): pl.pallas_call(kernel, in_specs=([SMEM] if scalar else []) + [VMEM] * (le...  12.3 us
    all_to_all x1, starting transfers between devices, per_device(): sums = lax.all_to_all(sums, REST, 0, 0)  11.8 us
    ppermute x1, waiting for transfers between devices, per_device(): lax.ppermute(own, SEQ, [(i, (i + SPAN) % seq) for i in range(seq)])  9.28 us
    all_to_all x1, waiting for transfers between devices, per_device(): sums = lax.all_to_all(sums, REST, 0, 0)  5.7 us
    ppermute x1, starting transfers between devices, per_device(): back = lax.ppermute(prev, SEQ, [((i + SPAN) % seq, i) for i in range(seq)])  4.55 us
    ppermute x1, starting transfers between devices, per_device(): lax.ppermute(own, SEQ, [(i, (i + SPAN) % seq) for i in range(seq)])  4.27 us
  transfers between devices with their start and end apart: 3, of which 2 were waited for; matrix products, arithmetic and copies ran while one was open for 0% of the time, Pallas kernels for 5%

profile of v2, /device:TPU:8, one launch (start us, length us, event | category | flops | bytes accessed | tf_op | source)
XLA Modules:
  0.0 81.2 jit_solution(15995106807437258554)
XLA Ops:
  0.6 0.7 convert_element_type.3
  1.3 0.8 pad_maximum_fusion.own_ref
  2.1 4.3 %collective-permute-start = (bf16[272,128]{1,0:T(8,128)(2,1)S(1)}, bf16[272,128]{1,0:T(8,128)(2,1)S(1)}, u32[]{:S(2)}, u32[]{:S(2)}) collective-permute-start(bf16[272,128]{1,0:T(8,128)(2,1)S(1)} %pad_maximum_fusion.own_ref), channel_id=1, source_target_pairs={{0,32},{4,36},{8,40},{12,44},{16,48},{20,52},{24,56},{28,60},{32,6... | collective-permute-start | bytes 208904 | tf_op jit(solution)/shard_map/ppermute | solution.py:247
  6.4 0.0 copy-start.4
  6.4 0.0 copy-start.5
  6.4 0.6 copy-done.4
  7.0 0.0 copy-done.5
  7.0 0.0 copy-start.1
  7.0 1.0 %copy-done.1 = bf16[128,2048]{1,0:T(8,128)(2,1)S(1)} copy-done((bf16[128,2048]{1,0:T(8,128)(2,1)S(1)}, bf16[128,2048]{1,0:T(8,128)(2,1)}, u32[]{:S(2)}) %copy-start.1) | copy-done | bytes 524312
  8.1 0.0 copy-start.2
  8.1 1.0 %copy-done.2 = bf16[128,2048]{1,0:T(8,128)(2,1)S(1)} copy-done((bf16[128,2048]{1,0:T(8,128)(2,1)S(1)}, bf16[128,2048]{1,0:T(8,128)(2,1)}, u32[]{:S(2)}) %copy-start.2) | copy-done | bytes 524312
  9.1 0.4 prepare_queries.1
  9.5 9.3 %collective-permute-done = bf16[272,128]{1,0:T(8,128)(2,1)S(1)} collective-permute-done((bf16[272,128]{1,0:T(8,128)(2,1)S(1)}, bf16[272,128]{1,0:T(8,128)(2,1)S(1)}, u32[]{:S(2)}, u32[]{:S(2)}) %collective-permute-start) | collective-permute-done | bytes 69664 | tf_op jit(solution)/shard_map/ppermute | solution.py:247
  18.8 0.1 broadcast_select_fusion
  18.9 14.7 %all_to_all.15.win_ref = bf16[8,272,128]{2,1,0:T(8,128)(2,1)S(1)} all-to-all(bf16[8,272,128]{2,1,0:T(8,128)(2,1)S(1)} %broadcast_select_fusion), channel_id=1, replica_groups=mesh['yl'=2,'z'=12,'core'=2,'ep'=4,'tp'=4] {'core','ep'}, dimensions={0} | all-to-all | bytes 1114112 | tf_op jit(solution)/shard_map/all_to_all | solution.py:256
  33.6 7.3 %attention_backward.1 = (bf16[8,272,128]{2,1,0:T(8,128)(2,1)S(1)}, f32[128,2048]{1,0:T(8,128)S(1)}) custom-call(s32[1]{0:T(128)} %bitcast.here_ref, bf16[2048,128]{1,0:T(8,128)(2,1)S(1)} %get-tuple-element.22.qn_ref, bf16[2048,128]{1,0:T(8,128)(2,1)S(1)} %get-tuple-element.23.g_ref, bf16[8,272,128]{2,1,0:T(8,128)(2,1)S(1)} %all_to_all.15.win_ref, ...), custom_call_target="tpu_custom_call" | custom-call | flops 4000000000 | bytes 10000000 | tf_op jit(solution)/shard_map/attention_backward/pallas_call | solution.py:227
  40.9 12.9 %all_to_all.16.parts_ref = bf16[8,272,128]{2,1,0:T(8,128)(2,1)S(1)} all-to-all(bf16[8,272,128]{2,1,0:T(8,128)(2,1)S(1)} %get-tuple-element.27), channel_id=1, replica_groups=mesh['yl'=2,'z'=12,'core'=2,'ep'=4,'tp'=4] {'core','ep'}, dimensions={0} | all-to-all | bytes 1114112 | tf_op jit(solution)/shard_map/all_to_all | solution.py:276
  53.9 0.0 copy-start.3
  53.9 0.7 combine_partials.1
  54.6 11.8 %all-to-all-start.2 = ((f32[96,2,128]{2,1,0:T(2,128)}), f32[96,2,128]{2,1,0:T(2,128)S(1)}, u32[]{:S(2)}, u32[]{:S(2)}) async-start(f32[96,2,128]{2,1,0:T(2,128)} %get-tuple-element.32), calls=%async_computation.2 | async-start | bytes 196608 | tf_op jit(solution)/shard_map/all_to_all | solution.py:287
  66.4 4.6 %collective-permute-start.1 = (bf16[256,128]{1,0:T(8,128)(2,1)S(1)}, bf16[256,128]{1,0:T(8,128)(2,1)S(1)}, u32[]{:S(2)}, u32[]{:S(2)}) collective-permute-start(bf16[256,128]{1,0:T(8,128)(2,1)S(1)} %get-tuple-element.29), channel_id=1, source_target_pairs={{32,0},{36,4},{40,8},{44,12},{48,16},{52,20},{56,24},{60,28},{64,3... | collective-permute-start | bytes 196616 | tf_op jit(solution)/shard_map/ppermute | solution.py:286
  70.9 0.0 copy-done.3
  71.0 0.0 copy-start
  71.0 3.1 %finish_queries.1 = bf16[128,2048]{1,0:T(8,128)(2,1)} custom-call(f32[128,2048]{1,0:T(8,128)S(1)} %get-tuple-element.26.dqt_ref, bf16[128,2048]{1,0:T(8,128)(2,1)S(1)} %copy-done.3, f32[1,128]{1,0:T(1,128)S(1)} %bitcast.8), custom_call_target="tpu_custom_call" | custom-call | flops 1000000000 | bytes 2000000 | tf_op jit(solution)/shard_map/finish_queries/pallas_call | solution.py:227
  74.0 0.0 collective-permute-done.1.back_ref
  74.0 0.0 copy-done
  74.0 0.8 finish_keys.1
  74.8 5.7 %all-to-all-done.2 = f32[96,2,128]{2,1,0:T(2,128)S(1)} async-done(((f32[96,2,128]{2,1,0:T(2,128)}), f32[96,2,128]{2,1,0:T(2,128)S(1)}, u32[]{:S(2)}, u32[]{:S(2)}) %all-to-all-start.2) | async-done | bytes 98336 | tf_op jit(solution)/shard_map/all_to_all | solution.py:287
  80.5 0.1 reduce_sum.9
  80.7 0.5 slice_bitcast_fusion
  (3 shorter events, 0.0 us)
Async XLA Ops:
  2.1 16.7 %collective-permute-start = (bf16[272,128]{1,0:T(8,128)(2,1)S(1)}, bf16[272,128]{1,0:T(8,128)(2,1)S(1)}, u32[]{:S(2)}, u32[]{:S(2)}) collective-permute-start(bf16[272,128]{1,0:T(8,128)(2,1)S(1)} %pad_maximum_fusion.own_ref), channel_id=1, source_target_pairs={{0,32},{4,36},{8,40},{12,44},{16,48},{20,52},{24,56},{28,60},{32,6... | collective-permute-start | bytes 208904 | tf_op jit(solution)/shard_map/ppermute | solution.py:247
  6.4 0.7 copy-start.4
  6.4 0.7 copy-start.5
  7.0 1.0 %copy-start.1 = (bf16[128,2048]{1,0:T(8,128)(2,1)S(1)}, bf16[128,2048]{1,0:T(8,128)(2,1)}, u32[]{:S(2)}) copy-start(bf16[128,2048]{1,0:T(8,128)(2,1)} %g_ref.1) | copy-start | bytes 1572868
  8.1 1.0 %copy-start.2 = (bf16[128,2048]{1,0:T(8,128)(2,1)S(1)}, bf16[128,2048]{1,0:T(8,128)(2,1)}, u32[]{:S(2)}) copy-start(bf16[128,2048]{1,0:T(8,128)(2,1)} %q_ref.3) | copy-start | bytes 1572868
  53.9 17.1 %copy-start.3 = (bf16[128,2048]{1,0:T(8,128)(2,1)S(1)}, bf16[128,2048]{1,0:T(8,128)(2,1)}, u32[]{:S(2)}) copy-start(bf16[128,2048]{1,0:T(8,128)(2,1)} %q_ref.3) | copy-start | bytes 1572868
  54.6 26.0 %all-to-all-start.2 = ((f32[96,2,128]{2,1,0:T(2,128)}), f32[96,2,128]{2,1,0:T(2,128)S(1)}, u32[]{:S(2)}, u32[]{:S(2)}) async-start(f32[96,2,128]{2,1,0:T(2,128)} %get-tuple-element.32), calls=%async_computation.2 | async-start | bytes 196608 | tf_op jit(solution)/shard_map/all_to_all | solution.py:287
  66.4 7.7 %collective-permute-start.1 = (bf16[256,128]{1,0:T(8,128)(2,1)S(1)}, bf16[256,128]{1,0:T(8,128)(2,1)S(1)}, u32[]{:S(2)}, u32[]{:S(2)}) collective-permute-start(bf16[256,128]{1,0:T(8,128)(2,1)S(1)} %get-tuple-element.29), channel_id=1, source_target_pairs={{32,0},{36,4},{40,8},{44,12},{48,16},{52,20},{56,24},{60,28},{64,3... | collective-permute-start | bytes 196616 | tf_op jit(solution)/shard_map/ppermute | solution.py:286
  71.0 3.1 %copy-start = (bf16[128,128]{1,0:T(8,128)(2,1)S(1)}, bf16[128,128]{1,0:T(8,128)(2,1)}, u32[]{:S(2)}) copy-start(bf16[128,128]{1,0:T(8,128)(2,1)} %key_ref.1) | copy-start | bytes 98308

commit v3 on v2

--- a/solution.py
+++ b/solution.py
@@ -1,3 +1,4 @@
+import functools
 import math
 
 import jax
@@ -88,17 +89,18 @@
     key_row = lax.broadcasted_iota(jnp.int32, (ROWS, ROWS), 0)
     query_col = lax.broadcasted_iota(jnp.int32, (ROWS, ROWS), 1)
     seg_q = jnp.broadcast_to(own_ref[2 * ROWS :, :].astype(F32)[0:1, :], (ROWS, ROWS))
+    last = 2 * ROWS + EXTRA
+    marks = [win_ref[p, 2 * ROWS : last, :].astype(F32)[0:1, :] for p in range(SPAN)]
+    marks = jnp.concatenate(marks, axis=0).T
     for p in range(SPAN):
         rows = slice(p * ROWS, (p + 1) * ROWS)
         unit, _ = unit_of(win_ref[p, :ROWS, :].astype(F32))
-        normed = unit * kgain
-        kn[rows, :] = normed.astype(BF16)
-        knt[:, rows] = normed.T.astype(BF16)
+        normed = (unit * kgain).astype(BF16)
+        kn[rows, :] = normed
+        knt[:, rows] = normed.T
         vals[rows, :] = win_ref[p, ROWS : 2 * ROWS, :]
-        marks = win_ref[p, 2 * ROWS : 2 * ROWS + EXTRA, :].astype(F32)[0:1, :]
-        seg_k = jnp.broadcast_to(marks, (ROWS, ROWS)).T
         late = jnp.where(here == p, 1, 0) * key_row > query_col
-        hidden = jnp.logical_or(seg_k != seg_q, late)
+        hidden = jnp.logical_or(marks[:, p : p + 1] != seg_q, late)
         bias[rows, :] = jnp.where(hidden, NEG, 0.0)
 
     blocks = [slice(p * ROWS, (p + 1) * ROWS) for p in range(SPAN)]
@@ -110,13 +112,14 @@
         for rows in blocks:
             hide = jnp.concatenate([bias[rows, :]] * (WIDE // ROWS), axis=1)
             s = dot_nt(kn[rows, :], qn_ref[cols, :]) + hide
+            s = s * EXP2_SCALE
             scores[slot, rows, :] = s
             top8 = jnp.maximum(top8, jnp.max(s.reshape(ROWS // 8, 8, WIDE), axis=0))
             yield
-        top = jnp.max(top8, axis=0, keepdims=True) * EXP2_SCALE
+        top = jnp.max(top8, axis=0, keepdims=True)
         total8 = jnp.zeros((8, WIDE), F32)
         for rows in blocks:
-            e = jnp.exp2(scores[slot, rows, :] * EXP2_SCALE - top)
+            e = jnp.exp2(scores[slot, rows, :] - top)
             scores[slot, rows, :] = e
             total8 = total8 + fold(e)
             yield
@@ -127,7 +130,9 @@
         inverse_total = 1.0 / totals[n]
         delta8 = jnp.zeros((8, WIDE), F32)
         for rows in blocks:
-            rounded = (scores[slot, rows, :] * inverse_total).astype(BF16)
+            prob = scores[slot, rows, :] * inverse_total
+            scores[slot, rows, :] = prob
+            rounded = prob.astype(BF16)
             probs_b[slot, rows, :] = rounded
             d = dot_nt(vals[rows, :], g_ref[cols, :])
             dprob[rows, :] = d
@@ -135,7 +140,7 @@
             yield
         delta = jnp.sum(delta8, axis=0, keepdims=True)
         for rows in blocks:
-            prob = scores[slot, rows, :] * inverse_total
+            prob = scores[slot, rows, :]
             dscore[slot, rows, :] = (prob * (dprob[rows, :] - delta)).astype(BF16)
             yield
 
@@ -190,7 +195,7 @@
         qgrad_ref[:, columns] = norm_backward(dq, unit, inverse, qgain).astype(BF16)
 
 
-def combine_kernel(here_ref, parts_ref, own_ref, prev_ref, sums_ref):
+def combine_kernel(factor, here_ref, parts_ref, own_ref, prev_ref, sums_ref):
     here = here_ref[0]
     for block in (0, 1):
         rows = slice(block * ROWS, (block + 1) * ROWS)
@@ -208,7 +213,7 @@
         extra = extra + parts_ref[p, 2 * ROWS :, :].astype(F32)
     qsum = extra[0:1, :] + extra[1:2, :]
     ksum = extra[2:3, :] + extra[3:4, :]
-    both = jnp.concatenate([qsum, ksum], axis=0)
+    both = jnp.concatenate([qsum, ksum], axis=0) * factor
     sums_ref[...] = jnp.broadcast_to(both[None], sums_ref.shape)
 
 
@@ -226,7 +231,7 @@
 def call(kernel, name, operands, outs, mib, scratch=(), flops=0, data=0, scalar=False):
     return pl.pallas_call(
         kernel,
-        in_specs=([SMEM] if scalar else []) + [VMEM] * (len(operands) - scalar),
+        in_specs=[SMEM] * scalar + [VMEM] * (len(operands) - scalar),
         out_specs=[VMEM] * len(outs),
         out_shape=[jax.ShapeDtypeStruct(*out) for out in outs],
         scratch_shapes=list(scratch),
@@ -236,27 +241,10 @@
     )(*operands)
 
 
-def per_device(queries, keys, value, gradient, segments, qgain, kgain):
-    here = lax.axis_index(ROW)
-    rest = lax.axis_size(REST)
-    seq = lax.axis_size(SEQ)
+def attention(*operands):
     heads = HEADS * ROWS
-    qgain, kgain = qgain.reshape(1, -1), kgain.reshape(1, -1)
-    marks = jnp.broadcast_to(segments.astype(BF16)[None], (EXTRA, ROWS))
-    own = jnp.concatenate([keys, value, marks], axis=0)
-    previous = lax.ppermute(own, SEQ, [(i, (i + SPAN) % seq) for i in range(seq)])
-    normed, gradient, gains = call(
-        prepare_kernel, "prepare_queries", (queries, gradient, qgain, kgain),
-        [((heads, HEAD_SIZE), BF16), ((heads, HEAD_SIZE), BF16), ((8, HEAD_SIZE), F32)],
-        4, flops=10**9, data=2 * 10**6,
-    )
-    previous, normed, gradient, gains = lax.optimization_barrier((previous, normed, gradient, gains))
-    is_own = jnp.arange(SPAN) >= here
-    outgoing = jnp.where(is_own[:, None, None], own[None], previous[None])
-    window = lax.all_to_all(outgoing, ROW, 0, 0)
-    place = here.astype(jnp.int32).reshape(1)
-    parts, dqt = call(
-        attention_kernel, "attention_backward", (place, normed, gradient, window, own, gains),
+    return call(
+        attention_kernel, "attention_backward", operands,
         [((SPAN, CHUNK, HEAD_SIZE), BF16), ((HEAD_SIZE, heads), F32)],
         16,
         scratch=[
@@ -273,13 +261,38 @@
         ],
         flops=4 * 10**9, data=10**7, scalar=True,
     )
+
+
+def per_device(queries, keys, value, gradient, segments, qgain, kgain):
+    here = lax.axis_index(ROW)
+    rest = lax.axis_size(REST)
+    seq = lax.axis_size(SEQ)
+    heads = HEADS * ROWS
+    qgain, kgain = qgain.reshape(1, -1), kgain.reshape(1, -1)
+    room = jnp.zeros((EXTRA, HEAD_SIZE), BF16)
+    own = jnp.concatenate([keys, value, room], axis=0)
+    own, segments = lax.optimization_barrier((own, segments))
+    own = own.at[2 * ROWS :].set(jnp.broadcast_to(segments.astype(BF16)[None], (EXTRA, ROWS)))
+    previous = lax.ppermute(own, SEQ, [(i, (i + SPAN) % seq) for i in range(seq)])
+    normed, gradient, gains = call(
+        prepare_kernel, "prepare_queries", (queries, gradient, qgain, kgain),
+        [((heads, HEAD_SIZE), BF16), ((heads, HEAD_SIZE), BF16), ((8, HEAD_SIZE), F32)],
+        4, flops=10**9, data=2 * 10**6,
+    )
+    previous, normed, gradient, gains = lax.optimization_barrier((previous, normed, gradient, gains))
+    is_own = jnp.arange(SPAN) >= here
+    outgoing = jnp.where(is_own[:, None, None], own[None], previous[None])
+    window = lax.all_to_all(outgoing, ROW, 0, 0)
+    place = here.astype(jnp.int32).reshape(1)
+    parts, dqt = attention(place, normed, gradient, window, own, gains)
     returned = lax.all_to_all(parts, ROW, 0, 0)
     (qgrad,) = call(
         finish_query_kernel, "finish_queries", (dqt, queries, qgain),
         [((ROWS, heads), BF16)], 4, flops=10**9, data=2 * 10**6,
     )
+    factor = 1.0 / math.sqrt(ROWS * seq * HEADS * lax.axis_size("tp"))
     mine, prev, sums = call(
-        combine_kernel, "combine_partials", (place, returned),
+        functools.partial(combine_kernel, factor), "combine_partials", (place, returned),
         [((2 * ROWS, HEAD_SIZE), F32), ((2 * ROWS, HEAD_SIZE), BF16), ((rest, 2, HEAD_SIZE), F32)],
         4, flops=10**8, data=10**6, scalar=True,
     )
@@ -289,8 +302,7 @@
         finish_key_kernel, "finish_keys", (mine, back, keys, kgain),
         [((ROWS, HEAD_SIZE), BF16), ((ROWS, HEAD_SIZE), BF16)], 4, flops=10**8, data=10**6,
     )
-    factor = 1.0 / math.sqrt(ROWS * seq * HEADS * lax.axis_size("tp"))
-    sums = jnp.sum(sums, axis=0) * factor
+    sums = jnp.sum(sums, axis=0)
     return qgrad, kgrad, vgrad, sums[0], sums[1]
 
 

time: 81.7 us -> 81.1 us (level)
    unnamed x12 -> x14, local copies, waits for them, and re-layouts: 2.75 us -> 2.76 us
where the time goes in v3:
time: 81.1 us; the launch traced here: 80.7 us
  blocking collectives  27.6 us (34%)
  starting transfers between devices  20.6 us (25%)
  waiting for transfers between devices  15 us (18%)
  Pallas kernels  12.2 us (15%)
  local copies, waits for them, and re-layouts  3.3 us (4%)
  other arithmetic  1.11 us (1%)
    all_to_all x1, blocking collectives, per_device(): window = lax.all_to_all(outgoing, ROW, 0, 0)  14.7 us
    all_to_all x1, blocking collectives, per_device(): returned = lax.all_to_all(parts, ROW, 0, 0)  12.9 us
    pallas_call x5, Pallas kernels, call(): pl.pallas_call(kernel, in_specs=[SMEM] * scalar + [VMEM] * (len(operands)...  12.2 us
    all_to_all x1, starting transfers between devices, per_device(): sums = lax.all_to_all(sums, REST, 0, 0)  11.8 us
    ppermute x1, waiting for transfers between devices, per_device(): lax.ppermute(own, SEQ, [(i, (i + SPAN) % seq) for i in range(seq)])  9.28 us
    all_to_all x1, waiting for transfers between devices, per_device(): sums = lax.all_to_all(sums, REST, 0, 0)  5.7 us
    ppermute x1, starting transfers between devices, per_device(): back = lax.ppermute(prev, SEQ, [((i + SPAN) % seq, i) for i in range(seq)])  4.55 us
    ppermute x1, starting transfers between devices, per_device(): lax.ppermute(own, SEQ, [(i, (i + SPAN) % seq) for i in range(seq)])  4.28 us
  transfers between devices with their start and end apart: 3, of which 2 were waited for; matrix products, arithmetic and copies ran while one was open for 0% of the time, Pallas kernels for 5%

profile of v3, /device:TPU:8, one launch (start us, length us, event | category | flops | bytes accessed | tf_op | source)
XLA Modules:
  0.0 80.7 jit_solution(8900028861813122898)
XLA Ops:
  0.7 0.0 copy-start.6
  0.7 0.9 %maximum_maximum_fusion = bf16[272,128]{1,0:T(8,128)(2,1)S(1)} fusion(bf16[128,128]{1,0:T(8,128)(2,1)} %param.11, bf16[128,128]{1,0:T(8,128)(2,1)} %key_ref.1, bf16[272]{0:T(512)(128)(2,1)S(1)} %pad.4.clone), kind=kLoop, calls=%fused_computation.1 | loop fusion | flops 208896 | bytes 135712 | tf_op jit(solution)/shard_map/concatenate | solution.py:273
  1.6 0.0 copy-done.6
  1.6 4.3 %collective-permute-start = (bf16[272,128]{1,0:T(8,128)(2,1)S(1)}, bf16[272,128]{1,0:T(8,128)(2,1)S(1)}, u32[]{:S(2)}, u32[]{:S(2)}) collective-permute-start(bf16[272,128]{1,0:T(8,128)(2,1)S(1)} %broadcast_dynamic-update-slice_fusion.own_ref), channel_id=1, source_target_pairs={{0,32},{4,36},{8,40},{12,44},{16,48},{20,52},{24,56},{28,60},{32,6... | collective-permute-start | bytes 208904 | tf_op jit(solution)/shard_map/ppermute | solution.py:276
  5.9 0.0 copy-start.4
  5.9 0.0 copy-start.5
  5.9 0.6 copy-done.4
  6.6 0.0 copy-done.5
  6.6 0.0 copy-start.1
  6.6 1.0 %copy-done.1 = bf16[128,2048]{1,0:T(8,128)(2,1)S(1)} copy-done((bf16[128,2048]{1,0:T(8,128)(2,1)S(1)}, bf16[128,2048]{1,0:T(8,128)(2,1)}, u32[]{:S(2)}) %copy-start.1) | copy-done | bytes 524312
  7.6 0.0 copy-start.2
  7.6 1.0 %copy-done.2 = bf16[128,2048]{1,0:T(8,128)(2,1)S(1)} copy-done((bf16[128,2048]{1,0:T(8,128)(2,1)S(1)}, bf16[128,2048]{1,0:T(8,128)(2,1)}, u32[]{:S(2)}) %copy-start.2) | copy-done | bytes 524312
  8.7 0.4 prepare_queries.1
  9.1 9.3 %collective-permute-done = bf16[272,128]{1,0:T(8,128)(2,1)S(1)} collective-permute-done((bf16[272,128]{1,0:T(8,128)(2,1)S(1)}, bf16[272,128]{1,0:T(8,128)(2,1)S(1)}, u32[]{:S(2)}, u32[]{:S(2)}) %collective-permute-start) | collective-permute-done | bytes 69664 | tf_op jit(solution)/shard_map/ppermute | solution.py:276
  18.3 0.1 broadcast_select_fusion
  18.5 14.7 %all_to_all.15.win_ref = bf16[8,272,128]{2,1,0:T(8,128)(2,1)S(1)} all-to-all(bf16[8,272,128]{2,1,0:T(8,128)(2,1)S(1)} %broadcast_select_fusion), channel_id=1, replica_groups=mesh['yl'=2,'z'=12,'core'=2,'ep'=4,'tp'=4] {'core','ep'}, dimensions={0} | all-to-all | bytes 1114112 | tf_op jit(solution)/shard_map/all_to_all | solution.py:285
  33.1 7.3 %attention_backward.1 = (bf16[8,272,128]{2,1,0:T(8,128)(2,1)S(1)}, f32[128,2048]{1,0:T(8,128)S(1)}) custom-call(s32[1]{0:T(128)} %bitcast.here_ref, bf16[2048,128]{1,0:T(8,128)(2,1)S(1)} %get-tuple-element.38.qn_ref, bf16[2048,128]{1,0:T(8,128)(2,1)S(1)} %get-tuple-element.39.g_ref, bf16[8,272,128]{2,1,0:T(8,128)(2,1)S(1)} %all_to_all.15.win_ref, ...), custom_call_target="tpu_custom_call" | custom-call | flops 4000000000 | bytes 10000000 | tf_op jit(solution)/shard_map/attention_backward/pallas_call | solution.py:232
  40.4 12.9 %all_to_all.16.parts_ref = bf16[8,272,128]{2,1,0:T(8,128)(2,1)S(1)} all-to-all(bf16[8,272,128]{2,1,0:T(8,128)(2,1)S(1)} %get-tuple-element.43), channel_id=1, replica_groups=mesh['yl'=2,'z'=12,'core'=2,'ep'=4,'tp'=4] {'core','ep'}, dimensions={0} | all-to-all | bytes 1114112 | tf_op jit(solution)/shard_map/all_to_all | solution.py:288
  53.4 0.0 copy-start.3
  53.4 0.7 combine_partials.1
  54.0 11.8 %all-to-all-start.2 = ((f32[96,2,128]{2,1,0:T(2,128)}), f32[96,2,128]{2,1,0:T(2,128)S(1)}, u32[]{:S(2)}, u32[]{:S(2)}) async-start(f32[96,2,128]{2,1,0:T(2,128)} %get-tuple-element.48), calls=%async_computation.2 | async-start | bytes 196608 | tf_op jit(solution)/shard_map/all_to_all | solution.py:300
  65.9 4.6 %collective-permute-start.1 = (bf16[256,128]{1,0:T(8,128)(2,1)S(1)}, bf16[256,128]{1,0:T(8,128)(2,1)S(1)}, u32[]{:S(2)}, u32[]{:S(2)}) collective-permute-start(bf16[256,128]{1,0:T(8,128)(2,1)S(1)} %get-tuple-element.45), channel_id=1, source_target_pairs={{32,0},{36,4},{40,8},{44,12},{48,16},{52,20},{56,24},{60,28},{64,3... | collective-permute-start | bytes 196616 | tf_op jit(solution)/shard_map/ppermute | solution.py:299
  70.4 0.0 copy-done.3
  70.4 0.0 copy-start
  70.4 3.1 %finish_queries.1 = bf16[128,2048]{1,0:T(8,128)(2,1)} custom-call(f32[128,2048]{1,0:T(8,128)S(1)} %get-tuple-element.42.dqt_ref, bf16[128,2048]{1,0:T(8,128)(2,1)S(1)} %copy-done.3, f32[1,128]{1,0:T(1,128)S(1)} %bitcast.8), custom_call_target="tpu_custom_call" | custom-call | flops 1000000000 | bytes 2000000 | tf_op jit(solution)/shard_map/finish_queries/pallas_call | solution.py:232
  73.5 0.0 collective-permute-done.1.back_ref
  73.5 0.0 copy-done
  73.5 0.8 finish_keys.1
  74.3 5.7 %all-to-all-done.2 = f32[96,2,128]{2,1,0:T(2,128)S(1)} async-done(((f32[96,2,128]{2,1,0:T(2,128)}), f32[96,2,128]{2,1,0:T(2,128)S(1)}, u32[]{:S(2)}, u32[]{:S(2)}) %all-to-all-start.2) | async-done | bytes 98336 | tf_op jit(solution)/shard_map/all_to_all | solution.py:300
  80.0 0.1 reduce_sum.9
  80.1 0.5 slice_bitcast_fusion
  (5 shorter events, 0.0 us)
Async XLA Ops:
  0.7 0.9 %copy-start.6 = (s32[128]{0:T(128)S(1)}, s32[128]{0:T(128)}, u32[]{:S(2)}) copy-start(s32[128]{0:T(128)} %param.13) | copy-start | bytes 1540
  1.6 16.8 %collective-permute-start = (bf16[272,128]{1,0:T(8,128)(2,1)S(1)}, bf16[272,128]{1,0:T(8,128)(2,1)S(1)}, u32[]{:S(2)}, u32[]{:S(2)}) collective-permute-start(bf16[272,128]{1,0:T(8,128)(2,1)S(1)} %broadcast_dynamic-update-slice_fusion.own_ref), channel_id=1, source_target_pairs={{0,32},{4,36},{8,40},{12,44},{16,48},{20,52},{24,56},{28,60},{32,6... | collective-permute-start | bytes 208904 | tf_op jit(solution)/shard_map/ppermute | solution.py:276
  5.9 0.7 copy-start.4
  5.9 0.7 copy-start.5
  6.6 1.0 %copy-start.1 = (bf16[128,2048]{1,0:T(8,128)(2,1)S(1)}, bf16[128,2048]{1,0:T(8,128)(2,1)}, u32[]{:S(2)}) copy-start(bf16[128,2048]{1,0:T(8,128)(2,1)} %g_ref.1) | copy-start | bytes 1572868
  7.6 1.0 %copy-start.2 = (bf16[128,2048]{1,0:T(8,128)(2,1)S(1)}, bf16[128,2048]{1,0:T(8,128)(2,1)}, u32[]{:S(2)}) copy-start(bf16[128,2048]{1,0:T(8,128)(2,1)} %q_ref.3) | copy-start | bytes 1572868
  53.4 17.0 %copy-start.3 = (bf16[128,2048]{1,0:T(8,128)(2,1)S(1)}, bf16[128,2048]{1,0:T(8,128)(2,1)}, u32[]{:S(2)}) copy-start(bf16[128,2048]{1,0:T(8,128)(2,1)} %q_ref.3) | copy-start | bytes 1572868
  54.0 26.0 %all-to-all-start.2 = ((f32[96,2,128]{2,1,0:T(2,128)}), f32[96,2,128]{2,1,0:T(2,128)S(1)}, u32[]{:S(2)}, u32[]{:S(2)}) async-start(f32[96,2,128]{2,1,0:T(2,128)} %get-tuple-element.48), calls=%async_computation.2 | async-start | bytes 196608 | tf_op jit(solution)/shard_map/all_to_all | solution.py:300
  65.9 7.7 %collective-permute-start.1 = (bf16[256,128]{1,0:T(8,128)(2,1)S(1)}, bf16[256,128]{1,0:T(8,128)(2,1)S(1)}, u32[]{:S(2)}, u32[]{:S(2)}) collective-permute-start(bf16[256,128]{1,0:T(8,128)(2,1)S(1)} %get-tuple-element.45), channel_id=1, source_target_pairs={{32,0},{36,4},{40,8},{44,12},{48,16},{52,20},{56,24},{60,28},{64,3... | collective-permute-start | bytes 196616 | tf_op jit(solution)/shard_map/ppermute | solution.py:299
  70.4 3.1 %copy-start = (bf16[128,128]{1,0:T(8,128)(2,1)S(1)}, bf16[128,128]{1,0:T(8,128)(2,1)}, u32[]{:S(2)}) copy-start(bf16[128,128]{1,0:T(8,128)(2,1)} %key_ref.1) | copy-start | bytes 98308

commit v4 on v3

--- a/solution.py
+++ b/solution.py
@@ -139,17 +139,22 @@
             delta8 = delta8 + fold(rounded.astype(F32) * d)
             yield
         delta = jnp.sum(delta8, axis=0, keepdims=True)
+        values = value_steps(n)
         for rows in blocks:
+            next(values, None)
             prob = scores[slot, rows, :]
             dscore[slot, rows, :] = (prob * (dprob[rows, :] - delta)).astype(BF16)
             yield
 
-    def sum_steps(n):
+    def value_steps(n):
         slot, cols = n % 2, slice(n * WIDE, (n + 1) * WIDE)
         for rows in (slice(0, TOKENS // 2), slice(TOKENS // 2, TOKENS)):
             v = dot_nn(probs_b[slot, rows, :], g_ref[cols, :])
             dv[rows, :] = v if n == 0 else dv[rows, :] + v
             yield
+
+    def sum_steps(n):
+        slot, cols = n % 2, slice(n * WIDE, (n + 1) * WIDE)
         for rows in (slice(0, TOKENS // 2), slice(TOKENS // 2, TOKENS)):
             k = dot_nn(dscore[slot, rows, :], qn_ref[cols, :])
             dk[rows, :] = k if n == 0 else dk[rows, :] + k
@@ -195,7 +200,7 @@
         qgrad_ref[:, columns] = norm_backward(dq, unit, inverse, qgain).astype(BF16)
 
 
-def combine_kernel(factor, here_ref, parts_ref, own_ref, prev_ref, sums_ref):
+def combine_kernel(here_ref, parts_ref, own_ref, prev_ref):
     here = here_ref[0]
     for block in (0, 1):
         rows = slice(block * ROWS, (block + 1) * ROWS)
@@ -208,6 +213,9 @@
             prev = prev + jnp.where(is_own, 0.0, part)
         own_ref[rows, :] = own
         prev_ref[rows, :] = prev.astype(BF16)
+
+
+def combine_sums_kernel(factor, parts_ref, sums_ref):
     extra = jnp.zeros((EXTRA, HEAD_SIZE), F32)
     for p in range(SPAN):
         extra = extra + parts_ref[p, 2 * ROWS :, :].astype(F32)
@@ -291,9 +299,13 @@
         [((ROWS, heads), BF16)], 4, flops=10**9, data=2 * 10**6,
     )
     factor = 1.0 / math.sqrt(ROWS * seq * HEADS * lax.axis_size("tp"))
-    mine, prev, sums = call(
-        functools.partial(combine_kernel, factor), "combine_partials", (place, returned),
-        [((2 * ROWS, HEAD_SIZE), F32), ((2 * ROWS, HEAD_SIZE), BF16), ((rest, 2, HEAD_SIZE), F32)],
+    (sums,) = call(
+        functools.partial(combine_sums_kernel, factor), "combine_sums", (returned,),
+        [((rest, 2, HEAD_SIZE), F32)], 4, data=10**5,
+    )
+    mine, prev = call(
+        combine_kernel, "combine_partials", (place, returned),
+        [((2 * ROWS, HEAD_SIZE), F32), ((2 * ROWS, HEAD_SIZE), BF16)],
         4, flops=10**8, data=10**6, scalar=True,
     )
     back = lax.ppermute(prev, SEQ, [((i + SPAN) % seq, i) for i in range(seq)])

time: 81.1 us -> 81.4 us (level)
    pallas_call x5 -> x6, Pallas kernels: 12.2 us -> 12.6 us  [call(): pl.pallas_call(kernel, in_specs=[SMEM] * scalar + [VMEM] * (len(operands)...]
  transfers between devices with their start and end apart: 3 -> 3, of which waited for: 2 -> 2; matrix products, arithmetic and copies ran while one was open for 0% -> 0% of each run, Pallas kernels for 5% -> 6%
where the time goes in v4:
time: 81.4 us; the launch traced here: 81 us
  blocking collectives  27.6 us (34%)
  starting transfers between devices  20.8 us (26%)
  waiting for transfers between devices  14.8 us (18%)
  Pallas kernels  12.6 us (15%)
  local copies, waits for them, and re-layouts  3.3 us (4%)
  other arithmetic  1.11 us (1%)
    all_to_all x1, blocking collectives, per_device(): window = lax.all_to_all(outgoing, ROW, 0, 0)  14.7 us
    all_to_all x1, blocking collectives, per_device(): returned = lax.all_to_all(parts, ROW, 0, 0)  13 us
    pallas_call x6, Pallas kernels, call(): pl.pallas_call(kernel, in_specs=[SMEM] * scalar + [VMEM] * (len(operands)...  12.6 us
    all_to_all x1, starting transfers between devices, per_device(): sums = lax.all_to_all(sums, REST, 0, 0)  11.9 us
    ppermute x1, waiting for transfers between devices, per_device(): lax.ppermute(own, SEQ, [(i, (i + SPAN) % seq) for i in range(seq)])  9.28 us
    all_to_all x1, waiting for transfers between devices, per_device(): sums = lax.all_to_all(sums, REST, 0, 0)  5.49 us
    ppermute x1, starting transfers between devices, per_device(): back = lax.ppermute(prev, SEQ, [((i + SPAN) % seq, i) for i in range(seq)])  4.55 us
    ppermute x1, starting transfers between devices, per_device(): lax.ppermute(own, SEQ, [(i, (i + SPAN) % seq) for i in range(seq)])  4.28 us
  transfers between devices with their start and end apart: 3, of which 2 were waited for; matrix products, arithmetic and copies ran while one was open for 0% of the time, Pallas kernels for 6%

profile of v4, /device:TPU:8, one launch (start us, length us, event | category | flops | bytes accessed | tf_op | source)
XLA Modules:
  0.0 81.0 jit_solution(15912256029294658787)
XLA Ops:
  0.7 0.0 copy-start.6
  0.7 0.9 %maximum_maximum_fusion = bf16[272,128]{1,0:T(8,128)(2,1)S(1)} fusion(bf16[128,128]{1,0:T(8,128)(2,1)} %param.11, bf16[128,128]{1,0:T(8,128)(2,1)} %key_ref.1, bf16[272]{0:T(512)(128)(2,1)S(1)} %pad.4.clone), kind=kLoop, calls=%fused_computation.1 | loop fusion | flops 208896 | bytes 135712 | tf_op jit(solution)/shard_map/concatenate | solution.py:281
  1.6 0.0 copy-done.6
  1.6 4.3 %collective-permute-start = (bf16[272,128]{1,0:T(8,128)(2,1)S(1)}, bf16[272,128]{1,0:T(8,128)(2,1)S(1)}, u32[]{:S(2)}, u32[]{:S(2)}) collective-permute-start(bf16[272,128]{1,0:T(8,128)(2,1)S(1)} %broadcast_dynamic-update-slice_fusion.own_ref), channel_id=1, source_target_pairs={{0,32},{4,36},{8,40},{12,44},{16,48},{20,52},{24,56},{28,60},{32,6... | collective-permute-start | bytes 208904 | tf_op jit(solution)/shard_map/ppermute | solution.py:284
  5.9 0.0 copy-start.4
  5.9 0.0 copy-start.5
  5.9 0.6 copy-done.4
  6.6 0.0 copy-done.5
  6.6 0.0 copy-start.1
  6.6 1.0 %copy-done.1 = bf16[128,2048]{1,0:T(8,128)(2,1)S(1)} copy-done((bf16[128,2048]{1,0:T(8,128)(2,1)S(1)}, bf16[128,2048]{1,0:T(8,128)(2,1)}, u32[]{:S(2)}) %copy-start.1) | copy-done | bytes 524312
  7.6 0.0 copy-start.2
  7.6 1.0 %copy-done.2 = bf16[128,2048]{1,0:T(8,128)(2,1)S(1)} copy-done((bf16[128,2048]{1,0:T(8,128)(2,1)S(1)}, bf16[128,2048]{1,0:T(8,128)(2,1)}, u32[]{:S(2)}) %copy-start.2) | copy-done | bytes 524312
  8.7 0.4 prepare_queries.1
  9.1 9.3 %collective-permute-done = bf16[272,128]{1,0:T(8,128)(2,1)S(1)} collective-permute-done((bf16[272,128]{1,0:T(8,128)(2,1)S(1)}, bf16[272,128]{1,0:T(8,128)(2,1)S(1)}, u32[]{:S(2)}, u32[]{:S(2)}) %collective-permute-start) | collective-permute-done | bytes 69664 | tf_op jit(solution)/shard_map/ppermute | solution.py:284
  18.3 0.1 broadcast_select_fusion
  18.5 14.7 %all_to_all.15.win_ref = bf16[8,272,128]{2,1,0:T(8,128)(2,1)S(1)} all-to-all(bf16[8,272,128]{2,1,0:T(8,128)(2,1)S(1)} %broadcast_select_fusion), channel_id=1, replica_groups=mesh['yl'=2,'z'=12,'core'=2,'ep'=4,'tp'=4] {'core','ep'}, dimensions={0} | all-to-all | bytes 1114112 | tf_op jit(solution)/shard_map/all_to_all | solution.py:293
  33.1 7.5 %attention_backward.1 = (bf16[8,272,128]{2,1,0:T(8,128)(2,1)S(1)}, f32[128,2048]{1,0:T(8,128)S(1)}) custom-call(s32[1]{0:T(128)} %bitcast.here_ref, bf16[2048,128]{1,0:T(8,128)(2,1)S(1)} %get-tuple-element.37.qn_ref, bf16[2048,128]{1,0:T(8,128)(2,1)S(1)} %get-tuple-element.38.g_ref, bf16[8,272,128]{2,1,0:T(8,128)(2,1)S(1)} %all_to_all.15.win_ref, ...), custom_call_target="tpu_custom_call" | custom-call | flops 4000000000 | bytes 10000000 | tf_op jit(solution)/shard_map/attention_backward/pallas_call | solution.py:240
  40.6 13.0 %all_to_all.16.parts_ref = bf16[8,272,128]{2,1,0:T(8,128)(2,1)S(1)} all-to-all(bf16[8,272,128]{2,1,0:T(8,128)(2,1)S(1)} %get-tuple-element.42), channel_id=1, replica_groups=mesh['yl'=2,'z'=12,'core'=2,'ep'=4,'tp'=4] {'core','ep'}, dimensions={0} | all-to-all | bytes 1114112 | tf_op jit(solution)/shard_map/all_to_all | solution.py:296
  53.5 0.7 combine_sums.1
  54.2 0.0 copy-start.3
  54.2 11.9 %all-to-all-start.2 = ((f32[96,2,128]{2,1,0:T(2,128)}), f32[96,2,128]{2,1,0:T(2,128)S(1)}, u32[]{:S(2)}, u32[]{:S(2)}) async-start(f32[96,2,128]{2,1,0:T(2,128)} %combine_sums.1), calls=%async_computation.2 | async-start | bytes 196608 | tf_op jit(solution)/shard_map/all_to_all | solution.py:312
  66.2 0.2 combine_partials.1
  66.4 4.6 %collective-permute-start.1 = (bf16[256,128]{1,0:T(8,128)(2,1)S(1)}, bf16[256,128]{1,0:T(8,128)(2,1)S(1)}, u32[]{:S(2)}, u32[]{:S(2)}) collective-permute-start(bf16[256,128]{1,0:T(8,128)(2,1)S(1)} %get-tuple-element.44), channel_id=1, source_target_pairs={{32,0},{36,4},{40,8},{44,12},{48,16},{52,20},{56,24},{60,28},{64,3... | collective-permute-start | bytes 196616 | tf_op jit(solution)/shard_map/ppermute | solution.py:311
  70.9 0.0 copy-done.3
  70.9 0.0 copy-start
  71.0 3.1 %finish_queries.1 = bf16[128,2048]{1,0:T(8,128)(2,1)} custom-call(f32[128,2048]{1,0:T(8,128)S(1)} %get-tuple-element.41.dqt_ref, bf16[128,2048]{1,0:T(8,128)(2,1)S(1)} %copy-done.3, f32[1,128]{1,0:T(1,128)S(1)} %bitcast.8), custom_call_target="tpu_custom_call" | custom-call | flops 1000000000 | bytes 2000000 | tf_op jit(solution)/shard_map/finish_queries/pallas_call | solution.py:240
  74.0 0.0 collective-permute-done.1.back_ref
  74.0 0.0 copy-done
  74.0 0.8 finish_keys.1
  74.8 5.5 %all-to-all-done.2 = f32[96,2,128]{2,1,0:T(2,128)S(1)} async-done(((f32[96,2,128]{2,1,0:T(2,128)}), f32[96,2,128]{2,1,0:T(2,128)S(1)}, u32[]{:S(2)}, u32[]{:S(2)}) %all-to-all-start.2) | async-done | bytes 98336 | tf_op jit(solution)/shard_map/all_to_all | solution.py:312
  80.3 0.1 reduce_sum.9
  80.4 0.5 slice_bitcast_fusion
  (5 shorter events, 0.0 us)
Async XLA Ops:
  0.7 0.9 %copy-start.6 = (s32[128]{0:T(128)S(1)}, s32[128]{0:T(128)}, u32[]{:S(2)}) copy-start(s32[128]{0:T(128)} %param.13) | copy-start | bytes 1540
  1.6 16.8 %collective-permute-start = (bf16[272,128]{1,0:T(8,128)(2,1)S(1)}, bf16[272,128]{1,0:T(8,128)(2,1)S(1)}, u32[]{:S(2)}, u32[]{:S(2)}) collective-permute-start(bf16[272,128]{1,0:T(8,128)(2,1)S(1)} %broadcast_dynamic-update-slice_fusion.own_ref), channel_id=1, source_target_pairs={{0,32},{4,36},{8,40},{12,44},{16,48},{20,52},{24,56},{28,60},{32,6... | collective-permute-start | bytes 208904 | tf_op jit(solution)/shard_map/ppermute | solution.py:284
  5.9 0.7 copy-start.4
  5.9 0.7 copy-start.5
  6.6 1.0 %copy-start.1 = (bf16[128,2048]{1,0:T(8,128)(2,1)S(1)}, bf16[128,2048]{1,0:T(8,128)(2,1)}, u32[]{:S(2)}) copy-start(bf16[128,2048]{1,0:T(8,128)(2,1)} %g_ref.1) | copy-start | bytes 1572868
  7.6 1.0 %copy-start.2 = (bf16[128,2048]{1,0:T(8,128)(2,1)S(1)}, bf16[128,2048]{1,0:T(8,128)(2,1)}, u32[]{:S(2)}) copy-start(bf16[128,2048]{1,0:T(8,128)(2,1)} %q_ref.3) | copy-start | bytes 1572868
  54.2 16.7 %copy-start.3 = (bf16[128,2048]{1,0:T(8,128)(2,1)S(1)}, bf16[128,2048]{1,0:T(8,128)(2,1)}, u32[]{:S(2)}) copy-start(bf16[128,2048]{1,0:T(8,128)(2,1)} %q_ref.3) | copy-start | bytes 1572868
  54.2 26.1 %all-to-all-start.2 = ((f32[96,2,128]{2,1,0:T(2,128)}), f32[96,2,128]{2,1,0:T(2,128)S(1)}, u32[]{:S(2)}, u32[]{:S(2)}) async-start(f32[96,2,128]{2,1,0:T(2,128)} %combine_sums.1), calls=%async_computation.2 | async-start | bytes 196608 | tf_op jit(solution)/shard_map/all_to_all | solution.py:312
  66.4 7.7 %collective-permute-start.1 = (bf16[256,128]{1,0:T(8,128)(2,1)S(1)}, bf16[256,128]{1,0:T(8,128)(2,1)S(1)}, u32[]{:S(2)}, u32[]{:S(2)}) collective-permute-start(bf16[256,128]{1,0:T(8,128)(2,1)S(1)} %get-tuple-element.44), channel_id=1, source_target_pairs={{32,0},{36,4},{40,8},{44,12},{48,16},{52,20},{56,24},{60,28},{64,3... | collective-permute-start | bytes 196616 | tf_op jit(solution)/shard_map/ppermute | solution.py:311
  70.9 3.1 %copy-start = (bf16[128,128]{1,0:T(8,128)(2,1)S(1)}, bf16[128,128]{1,0:T(8,128)(2,1)}, u32[]{:S(2)}) copy-start(bf16[128,128]{1,0:T(8,128)(2,1)} %key_ref.1) | copy-start | bytes 98308

commit v5 on v4

--- a/solution.py
+++ b/solution.py
@@ -1,4 +1,3 @@
-import functools
 import math
 
 import jax
@@ -166,7 +165,7 @@
     for n in range(GROUPS):
         work = [gradient_steps(n)]
         if n + 1 < GROUPS:
-            work.append(softmax_steps(n + 1))
+            work.insert(0, softmax_steps(n + 1))
         if n:
             work.append(sum_steps(n - 1))
         interleave(*work)
@@ -213,16 +212,6 @@
             prev = prev + jnp.where(is_own, 0.0, part)
         own_ref[rows, :] = own
         prev_ref[rows, :] = prev.astype(BF16)
-
-
-def combine_sums_kernel(factor, parts_ref, sums_ref):
-    extra = jnp.zeros((EXTRA, HEAD_SIZE), F32)
-    for p in range(SPAN):
-        extra = extra + parts_ref[p, 2 * ROWS :, :].astype(F32)
-    qsum = extra[0:1, :] + extra[1:2, :]
-    ksum = extra[2:3, :] + extra[3:4, :]
-    both = jnp.concatenate([qsum, ksum], axis=0) * factor
-    sums_ref[...] = jnp.broadcast_to(both[None], sums_ref.shape)
 
 
 def finish_key_kernel(own_ref, back_ref, key_ref, kgain_ref, kgrad_ref, vgrad_ref):
@@ -299,10 +288,8 @@
         [((ROWS, heads), BF16)], 4, flops=10**9, data=2 * 10**6,
     )
     factor = 1.0 / math.sqrt(ROWS * seq * HEADS * lax.axis_size("tp"))
-    (sums,) = call(
-        functools.partial(combine_sums_kernel, factor), "combine_sums", (returned,),
-        [((rest, 2, HEAD_SIZE), F32)], 4, data=10**5,
-    )
+    extra = jnp.sum(returned[:, 2 * ROWS : 2 * ROWS + 4].astype(F32), axis=0) * factor
+    sums = jnp.broadcast_to((extra[0::2] + extra[1::2])[None], (rest, 2, HEAD_SIZE))
     mine, prev = call(
         combine_kernel, "combine_partials", (place, returned),
         [((2 * ROWS, HEAD_SIZE), F32), ((2 * ROWS, HEAD_SIZE), BF16)],

time: 81.4 us -> 81.2 us (level)
    pallas_call x6 -> x5, Pallas kernels: 12.6 us -> 11.8 us  [call(): pl.pallas_call(kernel, in_specs=[SMEM] * scalar + [VMEM] * (len(operands)...]
where the time goes in v5:
time: 81.2 us; the launch traced here: 80.8 us
  blocking collectives  27.6 us (34%)
  starting transfers between devices  20.6 us (25%)
  waiting for transfers between devices  14.8 us (18%)
  Pallas kernels  11.8 us (15%)
  local copies, waits for them, and re-layouts  4.02 us (5%)
  other arithmetic  1.14 us (1%)
    all_to_all x1, blocking collectives, per_device(): window = lax.all_to_all(outgoing, ROW, 0, 0)  14.7 us
    all_to_all x1, blocking collectives, per_device(): returned = lax.all_to_all(parts, ROW, 0, 0)  12.9 us
    all_to_all x1, starting transfers between devices, per_device(): sums = lax.all_to_all(sums, REST, 0, 0)  11.8 us
    pallas_call x5, Pallas kernels, call(): pl.pallas_call(kernel, in_specs=[SMEM] * scalar + [VMEM] * (len(operands)...  11.8 us
    ppermute x1, waiting for transfers between devices, per_device(): lax.ppermute(own, SEQ, [(i, (i + SPAN) % seq) for i in range(seq)])  9.28 us
    all_to_all x1, waiting for transfers between devices, per_device(): sums = lax.all_to_all(sums, REST, 0, 0)  5.49 us
    ppermute x1, starting transfers between devices, per_device(): back = lax.ppermute(prev, SEQ, [((i + SPAN) % seq, i) for i in range(seq)])  4.55 us
    ppermute x1, starting transfers between devices, per_device(): lax.ppermute(own, SEQ, [(i, (i + SPAN) % seq) for i in range(seq)])  4.28 us
  transfers between devices with their start and end apart: 3, of which 2 were waited for; matrix products, arithmetic and copies ran while one was open for 0% of the time, Pallas kernels for 6%

profile of v5, /device:TPU:8, one launch (start us, length us, event | category | flops | bytes accessed | tf_op | source)
XLA Modules:
  0.0 80.8 jit_solution(17436032904334286740)
XLA Ops:
  0.7 0.0 copy-start.6
  0.7 0.9 %maximum_maximum_fusion = bf16[272,128]{1,0:T(8,128)(2,1)S(1)} fusion(bf16[128,128]{1,0:T(8,128)(2,1)} %param.11, bf16[128,128]{1,0:T(8,128)(2,1)} %key_ref.1, bf16[272]{0:T(512)(128)(2,1)S(1)} %pad.4.clone), kind=kLoop, calls=%fused_computation.1 | loop fusion | flops 208896 | bytes 135712 | tf_op jit(solution)/shard_map/concatenate | solution.py:270
  1.6 0.0 copy-done.6
  1.6 4.3 %collective-permute-start = (bf16[272,128]{1,0:T(8,128)(2,1)S(1)}, bf16[272,128]{1,0:T(8,128)(2,1)S(1)}, u32[]{:S(2)}, u32[]{:S(2)}) collective-permute-start(bf16[272,128]{1,0:T(8,128)(2,1)S(1)} %broadcast_dynamic-update-slice_fusion.own_ref), channel_id=1, source_target_pairs={{0,32},{4,36},{8,40},{12,44},{16,48},{20,52},{24,56},{28,60},{32,6... | collective-permute-start | bytes 208904 | tf_op jit(solution)/shard_map/ppermute | solution.py:273
  5.9 0.0 copy-start.4
  5.9 0.0 copy-start.5
  5.9 0.6 copy-done.4
  6.6 0.0 copy-done.5
  6.6 0.0 copy-start.1
  6.6 1.0 %copy-done.1 = bf16[128,2048]{1,0:T(8,128)(2,1)S(1)} copy-done((bf16[128,2048]{1,0:T(8,128)(2,1)S(1)}, bf16[128,2048]{1,0:T(8,128)(2,1)}, u32[]{:S(2)}) %copy-start.1) | copy-done | bytes 524312
  7.6 0.0 copy-start.2
  7.6 1.0 %copy-done.2 = bf16[128,2048]{1,0:T(8,128)(2,1)S(1)} copy-done((bf16[128,2048]{1,0:T(8,128)(2,1)S(1)}, bf16[128,2048]{1,0:T(8,128)(2,1)}, u32[]{:S(2)}) %copy-start.2) | copy-done | bytes 524312
  8.7 0.4 prepare_queries.1
  9.1 9.3 %collective-permute-done = bf16[272,128]{1,0:T(8,128)(2,1)S(1)} collective-permute-done((bf16[272,128]{1,0:T(8,128)(2,1)S(1)}, bf16[272,128]{1,0:T(8,128)(2,1)S(1)}, u32[]{:S(2)}, u32[]{:S(2)}) %collective-permute-start) | collective-permute-done | bytes 69664 | tf_op jit(solution)/shard_map/ppermute | solution.py:273
  18.3 0.1 broadcast_select_fusion
  18.5 14.7 %all_to_all.15.win_ref = bf16[8,272,128]{2,1,0:T(8,128)(2,1)S(1)} all-to-all(bf16[8,272,128]{2,1,0:T(8,128)(2,1)S(1)} %broadcast_select_fusion), channel_id=1, replica_groups=mesh['yl'=2,'z'=12,'core'=2,'ep'=4,'tp'=4] {'core','ep'}, dimensions={0} | all-to-all | bytes 1114112 | tf_op jit(solution)/shard_map/all_to_all | solution.py:282
  33.1 7.3 %attention_backward.1 = (bf16[8,272,128]{2,1,0:T(8,128)(2,1)S(1)}, f32[128,2048]{1,0:T(8,128)S(1)}) custom-call(s32[1]{0:T(128)} %bitcast.here_ref, bf16[2048,128]{1,0:T(8,128)(2,1)S(1)} %get-tuple-element.37.qn_ref, bf16[2048,128]{1,0:T(8,128)(2,1)S(1)} %get-tuple-element.38.g_ref, bf16[8,272,128]{2,1,0:T(8,128)(2,1)S(1)} %all_to_all.15.win_ref, ...), custom_call_target="tpu_custom_call" | custom-call | flops 4000000000 | bytes 10000000 | tf_op jit(solution)/shard_map/attention_backward/pallas_call | solution.py:229
  40.5 12.9 %all_to_all.16.parts_ref = bf16[8,272,128]{2,1,0:T(8,128)(2,1)S(1)} all-to-all(bf16[8,272,128]{2,1,0:T(8,128)(2,1)S(1)} %get-tuple-element.42), channel_id=1, replica_groups=mesh['yl'=2,'z'=12,'core'=2,'ep'=4,'tp'=4] {'core','ep'}, dimensions={0} | all-to-all | bytes 1114112 | tf_op jit(solution)/shard_map/all_to_all | solution.py:285
  53.4 0.0 copy-start.3
  53.5 0.7 broadcast_in_dim.44
  54.2 11.8 %all-to-all-start.2 = ((f32[96,2,128]{2,1,0:T(2,128)}), f32[96,2,128]{2,1,0:T(2,128)S(1)}, u32[]{:S(2)}, u32[]{:S(2)}) async-start(f32[96,2,128]{2,1,0:T(2,128)} %broadcast_in_dim.44), calls=%async_computation.2 | async-start | bytes 196608 | tf_op jit(solution)/shard_map/all_to_all | solution.py:299
  66.0 0.2 combine_partials.1
  66.2 4.6 %collective-permute-start.1 = (bf16[256,128]{1,0:T(8,128)(2,1)S(1)}, bf16[256,128]{1,0:T(8,128)(2,1)S(1)}, u32[]{:S(2)}, u32[]{:S(2)}) collective-permute-start(bf16[256,128]{1,0:T(8,128)(2,1)S(1)} %get-tuple-element.44), channel_id=1, source_target_pairs={{32,0},{36,4},{40,8},{44,12},{48,16},{52,20},{56,24},{60,28},{64,3... | collective-permute-start | bytes 196616 | tf_op jit(solution)/shard_map/ppermute | solution.py:298
  70.7 0.0 copy-done.3
  70.8 0.0 copy-start
  70.8 3.1 %finish_queries.1 = bf16[128,2048]{1,0:T(8,128)(2,1)} custom-call(f32[128,2048]{1,0:T(8,128)S(1)} %get-tuple-element.41.dqt_ref, bf16[128,2048]{1,0:T(8,128)(2,1)S(1)} %copy-done.3, f32[1,128]{1,0:T(1,128)S(1)} %bitcast.8), custom_call_target="tpu_custom_call" | custom-call | flops 1000000000 | bytes 2000000 | tf_op jit(solution)/shard_map/finish_queries/pallas_call | solution.py:229
  73.8 0.0 collective-permute-done.1.back_ref
  73.8 0.0 copy-done
  73.8 0.8 finish_keys.1
  74.6 5.5 %all-to-all-done.2 = f32[96,2,128]{2,1,0:T(2,128)S(1)} async-done(((f32[96,2,128]{2,1,0:T(2,128)}), f32[96,2,128]{2,1,0:T(2,128)S(1)}, u32[]{:S(2)}, u32[]{:S(2)}) %all-to-all-start.2) | async-done | bytes 98336 | tf_op jit(solution)/shard_map/all_to_all | solution.py:299
  80.1 0.1 reduce_sum.19
  80.2 0.5 slice_bitcast_fusion
  (10 shorter events, 0.1 us)
Async XLA Ops:
  0.7 0.9 %copy-start.6 = (s32[128]{0:T(128)S(1)}, s32[128]{0:T(128)}, u32[]{:S(2)}) copy-start(s32[128]{0:T(128)} %param.13) | copy-start | bytes 1540
  1.6 16.8 %collective-permute-start = (bf16[272,128]{1,0:T(8,128)(2,1)S(1)}, bf16[272,128]{1,0:T(8,128)(2,1)S(1)}, u32[]{:S(2)}, u32[]{:S(2)}) collective-permute-start(bf16[272,128]{1,0:T(8,128)(2,1)S(1)} %broadcast_dynamic-update-slice_fusion.own_ref), channel_id=1, source_target_pairs={{0,32},{4,36},{8,40},{12,44},{16,48},{20,52},{24,56},{28,60},{32,6... | collective-permute-start | bytes 208904 | tf_op jit(solution)/shard_map/ppermute | solution.py:273
  5.9 0.7 copy-start.4
  5.9 0.7 copy-start.5
  6.6 1.0 %copy-start.1 = (bf16[128,2048]{1,0:T(8,128)(2,1)S(1)}, bf16[128,2048]{1,0:T(8,128)(2,1)}, u32[]{:S(2)}) copy-start(bf16[128,2048]{1,0:T(8,128)(2,1)} %g_ref.1) | copy-start | bytes 1572868
  7.6 1.0 %copy-start.2 = (bf16[128,2048]{1,0:T(8,128)(2,1)S(1)}, bf16[128,2048]{1,0:T(8,128)(2,1)}, u32[]{:S(2)}) copy-start(bf16[128,2048]{1,0:T(8,128)(2,1)} %q_ref.3) | copy-start | bytes 1572868
  53.4 17.3 %copy-start.3 = (bf16[128,2048]{1,0:T(8,128)(2,1)S(1)}, bf16[128,2048]{1,0:T(8,128)(2,1)}, u32[]{:S(2)}) copy-start(bf16[128,2048]{1,0:T(8,128)(2,1)} %q_ref.3) | copy-start | bytes 1572868
  54.2 26.0 %all-to-all-start.2 = ((f32[96,2,128]{2,1,0:T(2,128)}), f32[96,2,128]{2,1,0:T(2,128)S(1)}, u32[]{:S(2)}, u32[]{:S(2)}) async-start(f32[96,2,128]{2,1,0:T(2,128)} %broadcast_in_dim.44), calls=%async_computation.2 | async-start | bytes 196608 | tf_op jit(solution)/shard_map/all_to_all | solution.py:299
  66.2 7.7 %collective-permute-start.1 = (bf16[256,128]{1,0:T(8,128)(2,1)S(1)}, bf16[256,128]{1,0:T(8,128)(2,1)S(1)}, u32[]{:S(2)}, u32[]{:S(2)}) collective-permute-start(bf16[256,128]{1,0:T(8,128)(2,1)S(1)} %get-tuple-element.44), channel_id=1, source_target_pairs={{32,0},{36,4},{40,8},{44,12},{48,16},{52,20},{56,24},{60,28},{64,3... | collective-permute-start | bytes 196616 | tf_op jit(solution)/shard_map/ppermute | solution.py:298
  70.8 3.1 %copy-start = (bf16[128,128]{1,0:T(8,128)(2,1)S(1)}, bf16[128,128]{1,0:T(8,128)(2,1)}, u32[]{:S(2)}) copy-start(bf16[128,128]{1,0:T(8,128)(2,1)} %key_ref.1) | copy-start | bytes 98308
